TPU v7x, 512 devices: a whole 4x4x16 slice. The times are simulated.
512 devices in a mesh: group: 4 (over y), ep: 128 (over x, z, core).
Axes of the slice: x: 4, y: 4, z: 16, core: 2. Of those that a mesh axis runs over, the one named last changes fastest.
Arguments:
- tokens: bfloat16 [4096, 3584], P('ep'), may hold values from -6 to 6
- expert_ids: int32 [4096, 8], P('ep'), may hold values from 0 to 63, all different within a row; in each aligned block of 8 rows (0 to 7, 8 to 15, ...) at most 2 rows name the same one
- route_weight: float32 [4096, 8], P('ep'), may hold values from 0.05 to 0.5
- w_gate: bfloat16 [128, 3584, 512], P('ep', None, 'group'), may hold values from -0.09375 to 0.09375
- w_up: bfloat16 [128, 3584, 512], P('ep', None, 'group'), may hold values from -0.09375 to 0.09375
- w_down: bfloat16 [128, 512, 3584], P('ep', 'group'), may hold values from -0.1875 to 0.1875
Outputs:
- moe_out: bfloat16 [4096, 3584], P('ep')
Inputs may be any that keep to these rules, and one draw needn't show every extreme that they name: `expert_ids`: in each aligned block of 8 rows no expert is named by more than 2 rows, a bound that some block reaches.
All inputs are finite; a program needn't handle non-finite values.
Results may differ from a plain program's by a relative error of at most 0.0057.
Values may be sent and summed in bfloat16 or wider, within the bound.
No kernel may reach another device: no remote copies, remote signals or barrier semaphores. Data moves between devices by JAX's collectives and lax.ppermute only.
A program may use at most 64 MiB of HBM per device.

v0:
```python
import jax
import jax.numpy as jnp
from jax import lax
from jax.sharding import PartitionSpec as P


def slot_layout(choice_ids, blocks, capacity, experts):
    tok_count, top_count = choice_ids.shape
    per_block = tok_count // blocks
    onehot = (
        choice_ids.reshape(blocks, per_block * top_count)[:, :, None]
        == jnp.arange(experts, dtype=jnp.int32)[None, None, :]
    ).astype(jnp.int32)
    before = jnp.cumsum(onehot, axis=1) - onehot
    rank_value = jnp.sum(before * onehot, axis=2)
    slot_index = (jnp.arange(blocks, dtype=jnp.int32)[:, None] * capacity + rank_value).reshape(
        tok_count, top_count
    )
    token_index = jnp.broadcast_to(
        jnp.arange(tok_count, dtype=jnp.int32)[:, None], (tok_count, top_count)
    )
    slot_table = (
        jnp.full((experts, blocks * capacity), tok_count, jnp.int32)
        .at[choice_ids, slot_index]
        .set(token_index)
    )
    return (slot_table, slot_index)


def combine(returned, choice_ids, slot_index, weights):
    devices, slots, features = returned.shape
    flat_rows = returned.reshape(devices * slots, features)
    first_index = 2 * choice_ids * slots + slot_index
    pair_sum = flat_rows[first_index].astype(jnp.float32) + flat_rows[first_index + slots].astype(
        jnp.float32
    )
    return jnp.sum(weights[:, :, None] * pair_sum, axis=1)


def per_device(tokens, expert_ids, route_weight, w_gate, w_up, w_down):
    groups = lax.axis_size("group")
    devices = lax.axis_size("ep")
    experts = devices // 2
    tok_count, top_count = expert_ids.shape
    per_block = tok_count // groups
    capacity = max(2, per_block * top_count * 2 // experts)
    features = tokens.shape[1]
    gate_local = w_gate[0]
    up_local = w_up[0]
    down_local = w_down[0]
    padded = jnp.concatenate([tokens, jnp.zeros((1, features), tokens.dtype)], 0)
    slot_table, slot_index = slot_layout(expert_ids, groups, capacity, experts)
    gathered = padded[slot_table]
    doubled = jnp.broadcast_to(gathered[:, None], (experts, 2) + gathered.shape[1:])
    received = lax.all_to_all(
        doubled.reshape(devices, slot_table.shape[1], features),
        "ep",
        split_axis=0,
        concat_axis=0,
        tiled=True,
    )
    sources, slots, _ = received.shape
    inputs = received.reshape(sources * slots, features)
    gate_value = jnp.dot(inputs, gate_local, preferred_element_type=jnp.float32)
    up_value = jnp.dot(inputs, up_local, preferred_element_type=jnp.float32)
    hidden = (jax.nn.silu(gate_value) * up_value).astype(jnp.bfloat16)
    partial_value = jnp.dot(hidden, down_local, preferred_element_type=jnp.float32).astype(
        jnp.bfloat16
    )
    returned = lax.all_to_all(
        partial_value.reshape(sources, slots, features),
        "ep",
        split_axis=0,
        concat_axis=0,
        tiled=True,
    )
    mixed_out = combine(returned, expert_ids, slot_index, route_weight)
    moe_out = lax.psum(mixed_out, "group").astype(jnp.bfloat16)
    return moe_out


def solution(mesh):
    in_specs = (
        P("ep", None),
        P("ep", None),
        P("ep", None),
        P("ep", None, "group"),
        P("ep", None, "group"),
        P("ep", "group", None),
    )
    out_specs = P("ep", None)
    return jax.shard_map(
        per_device, mesh=mesh, in_specs=in_specs, out_specs=out_specs, check_vma=False
    )
```

profile of v0, /device:TPU:6, one launch (start us, length us, event | category | flops | bytes accessed | tf_op | source)
XLA Modules:
  0.0 750.1 jit_solution(3571628648009542331)
XLA Ops:
  0.0 0.0 copy-start
  0.0 0.8 copy.9
  0.8 0.1 eq.15
  0.9 0.1 fusion.24
  1.0 0.1 reduce_window_sum.11
  1.2 0.2 select_reduce_fusion
  1.4 0.1 reduce_sum.23
  1.5 0.1 add.79
  1.6 0.1 add.80
  1.6 0.1 fusion.26
  1.7 0.1 reshape.94
  1.8 0.1 reshape.96
  1.9 0.0 copy-start.3
  2.0 11.3 %scatter_fusion = s32[64,8]{0,1:T(8,128)S(1)} fusion(s32[64,8]{0,1:T(8,128)S(1)} %broadcast_in_dim.14, s32[256]{0:T(256)S(1)} %reshape.94, s32[256]{0:T(256)S(1)} %reshape.96), kind=kCustom, calls=%fused_computation.3 | custom fusion | bytes 5120 | tf_op jit(solution)/shard_map/scatter | solution.py:25
  13.3 0.1 copy.13
  13.4 0.1 reshape.72
  13.5 0.0 copy-done.3
  13.5 4.2 gather_fusion
  17.7 2.6 broadcast_in_dim.36
  20.3 0.0 copy-start.5
  20.3 341.4 %all_to_all.10 = bf16[128,8,3584]{2,1,0:T(8,128)(2,1)S(1)} all-to-all(bf16[128,8,3584]{2,1,0:T(8,128)(2,1)S(1)} %bitcast.36), channel_id=1, replica_groups=mesh['group'=4,'ep'=128] {'ep'}, dimensions={0} | all-to-all | bytes 14680064 | tf_op jit(solution)/shard_map/all_to_all | solution.py:55
  361.7 0.0 copy-start.1
  361.7 3.0 copy-done.1
  364.7 0.0 copy-done.5
  364.7 0.0 copy-start.2
  364.7 2.1 fusion.2
  366.7 0.0 copy-done
  366.7 0.0 copy-done.2
  366.8 11.8 %fusion.4 = bf16[128,8,3584]{2,1,0:T(8,128)(2,1)} fusion(bf16[128,8,3584]{2,1,0:T(8,128)(2,1)} %copy-done.1, bf16[1,128,3584]{2,1,0:T(8,128)(2,1)S(1)} %copy-done, bf16[1,3584,128]{2,1,0:T(8,128)(2,1)S(1)} %copy-done.2, f32[1024,128]{1,0:T(8,128)S(1)} %fusion.2), kind=kOutput, calls=%fused_computation.9 | convolution fusion | flops 1883504640 | bytes 17039360 | tf_op jit(solution)/shard_map/dot_general | solution.py:67
  378.6 0.0 copy-start.4
  378.6 11.5 %all-to-all-start.1 = ((bf16[128,8,3584]{2,1,0:T(8,128)(2,1)}), bf16[128,8,3584]{2,1,0:T(8,128)(2,1)}, u32[]{:S(2)}, u32[]{:S(2)}) async-start(bf16[128,8,3584]{2,1,0:T(8,128)(2,1)} %fusion.4), calls=%async_computation.1 | async-start | bytes 14680064 | tf_op jit(solution)/shard_map/all_to_all | solution.py:70
  390.1 0.1 reduce_sum.24
  390.2 0.1 compare_select_fusion.1
  390.3 0.1 reshape.80
  390.4 0.1 reshape.88
  390.5 0.0 copy-done.4
  390.5 0.1 copy.8
  390.6 318.5 %all-to-all-done.1 = bf16[128,8,3584]{2,1,0:T(8,128)(2,1)} async-done(((bf16[128,8,3584]{2,1,0:T(8,128)(2,1)}), bf16[128,8,3584]{2,1,0:T(8,128)(2,1)}, u32[]{:S(2)}, u32[]{:S(2)}) %all-to-all-start.1) | async-done | bytes 7340064 | tf_op jit(solution)/shard_map/all_to_all | solution.py:70
  709.1 7.6 %gather_fusion.1 = bf16[256,3584]{1,0:T(8,128)(2,1)S(1)} fusion(bf16[1024,3584]{1,0:T(8,128)(2,1)} %bitcast.8, s32[1024]{0:T(1024)S(1)} %pad_clamp_fusion.1), kind=kCustom, calls=%fused_computation.1 | custom fusion | bytes 3671040 | tf_op jit(solution)/shard_map/gather | solution.py:34
  716.6 8.9 %gather_fusion.2 = bf16[256,3584]{1,0:T(8,128)(2,1)} fusion(bf16[1024,3584]{1,0:T(8,128)(2,1)} %bitcast.8, s32[1024]{0:T(1024)S(1)} %pad_clamp_fusion), kind=kCustom, calls=%fused_computation.2 | custom fusion | bytes 3671040 | tf_op jit(solution)/shard_map/gather | solution.py:34
  725.5 3.0 fusion.5
  728.6 21.6 %all-reduce.2 = bf16[32,3584]{1,0:T(8,128)(2,1)} all-reduce(f32[32,3584]{1,0:T(8,128)S(1)} %fusion.5), channel_id=1, replica_groups=mesh['group'=4,'ep'=128] {'group'}, use_global_device_ids=true, to_apply=%region_4.5 | all-reduce | flops 114688 | bytes 688128 | tf_op jit(solution)/shard_map/psum | solution.py:78
  (8 shorter events, 0.1 us)
Async XLA Ops:
  0.0 366.7 %copy-start = (bf16[1,128,3584]{2,1,0:T(8,128)(2,1)S(1)}, bf16[1,128,3584]{2,1,0:T(8,128)(2,1)}, u32[]{:S(2)}) copy-start(bf16[1,128,3584]{2,1,0:T(8,128)(2,1)} %param.11) | copy-start | bytes 2752516
  1.9 11.5 %copy-start.3 = (bf16[32,3584]{1,0:T(8,128)(2,1)S(1)}, bf16[32,3584]{1,0:T(8,128)(2,1)}, u32[]{:S(2)}) copy-start(bf16[32,3584]{1,0:T(8,128)(2,1)} %param.6) | copy-start | bytes 688132
  20.3 344.4 %copy-start.5 = (bf16[1,3584,128]{2,1,0:T(8,128)(2,1)S(1)}, bf16[1,3584,128]{2,1,0:T(8,128)(2,1)}, u32[]{:S(2)}) copy-start(bf16[1,3584,128]{2,1,0:T(8,128)(2,1)} %param.9) | copy-start | bytes 2752516
  361.7 3.0 copy-start.1
  364.7 2.1 copy-start.2
  378.6 11.9 %copy-start.4 = (f32[32,8]{0,1:T(8,128)S(1)}, f32[32,8]{0,1:T(8,128)}, u32[]{:S(2)}) copy-start(f32[32,8]{0,1:T(8,128)} %param.8) | copy-start | bytes 3076
  378.6 330.5 %all-to-all-start.1 = ((bf16[128,8,3584]{2,1,0:T(8,128)(2,1)}), bf16[128,8,3584]{2,1,0:T(8,128)(2,1)}, u32[]{:S(2)}, u32[]{:S(2)}) async-start(bf16[128,8,3584]{2,1,0:T(8,128)(2,1)} %fusion.4), calls=%async_computation.1 | async-start | bytes 14680064 | tf_op jit(solution)/shard_map/all_to_all | solution.py:70
where the time goes:
time: 755 us; the launch traced here: 750 us
  blocking collectives  363 us (48%)
  waiting for transfers between devices  318 us (42%)
  local copies, waits for them, and re-layouts  39.4 us (5%)
  matrix products  13.9 us (2%)
  starting transfers between devices  11.5 us (2%)
    all_to_all x1, blocking collectives, per_device(): lax.all_to_all(doubled.reshape(devices, slot_table.shape[1], features), '...  341 us
    all_to_all x1, waiting for transfers between devices, per_device(): lax.all_to_all(partial_value.reshape(sources, slots, features), 'ep', spl...  318 us
    psum x1, blocking collectives, per_device(): moe_out = lax.psum(mixed_out, 'group').astype(jnp.bfloat16)  21.6 us
  transfers between devices with their start and end apart: 1, of which 1 were waited for; matrix products, arithmetic and copies ran while one was open for 0% of the time, Pallas kernels for 0%

commit v1 on v0

v1 whole, which is shorter than its diff:
```python
import jax
import jax.numpy as jnp
from jax import lax
from jax.experimental import pallas as pl
from jax.experimental.pallas import tpu as pltpu
from jax.sharding import Mesh, PartitionSpec as P

BLOCK = 8
CAP = 2
SLOT = 8
MIB = 1 << 20


def params():
    return pltpu.CompilerParams(vmem_limit_bytes=24 * MIB)


def slot_mask(ids, experts):
    tokens, top = ids.shape
    lane = lax.broadcasted_iota(jnp.int32, (tokens, experts), 1)
    hit = jnp.zeros((tokens, experts), jnp.float32)
    for j in range(top):
        hit = hit + jnp.where(ids[:, j:j + 1] == lane, 1.0, 0.0)
    row = lax.broadcasted_iota(jnp.int32, (tokens, tokens), 0)
    col = lax.broadcasted_iota(jnp.int32, (tokens, tokens), 1)
    earlier = jnp.where((row // BLOCK == col // BLOCK) & (col < row), 1.0, 0.0).astype(jnp.bfloat16)
    rank = jnp.dot(earlier, hit.astype(jnp.bfloat16), preferred_element_type=jnp.float32)
    place = lax.broadcasted_iota(jnp.int32, (tokens, experts), 0) // BLOCK * CAP
    code = jnp.where(hit > 0.5, place.astype(jnp.float32) + rank + 1.0, 0.0)
    spread = expand(experts)
    wide = jnp.dot(code.astype(jnp.bfloat16), spread, preferred_element_type=jnp.float32)
    slot = lax.broadcasted_iota(jnp.int32, (tokens, experts * SLOT), 1) % SLOT
    return wide == (slot + 1).astype(jnp.float32)


def expand(experts):
    row = lax.broadcasted_iota(jnp.int32, (experts, experts * SLOT), 0)
    col = lax.broadcasted_iota(jnp.int32, (experts, experts * SLOT), 1)
    return jnp.where(col // SLOT == row, 1.0, 0.0).astype(jnp.bfloat16)


def dispatch_kernel(y_ref, ids_ref, tokens_ref, out_ref):
    experts = out_ref.shape[0] // SLOT
    onehot = jnp.where(slot_mask(ids_ref[...], experts), 1.0, 0.0).astype(jnp.bfloat16)
    rows = lax.dot_general(
        onehot, tokens_ref[...], (((0,), (0,)), ((), ())), preferred_element_type=jnp.float32
    )
    out_ref[...] = rows.astype(jnp.bfloat16)


def dispatch(y, ids, tokens, experts, width):
    count = tokens.shape[0]
    return pl.pallas_call(
        dispatch_kernel,
        grid_spec=pltpu.PrefetchScalarGridSpec(
            num_scalar_prefetch=1,
            grid=(1,),
            in_specs=[
                pl.BlockSpec(ids.shape, lambda i, y: (0, 0)),
                pl.BlockSpec((count, width), lambda i, y: (0, y[0])),
            ],
            out_specs=pl.BlockSpec((experts * SLOT, width), lambda i, y: (0, 0)),
        ),
        out_shape=jax.ShapeDtypeStruct((experts * SLOT, width), tokens.dtype),
        compiler_params=params(),
        name="dispatch_rows",
    )(y, ids, tokens)


def combine_kernel(y_ref, ids_ref, weight_ref, rows_ref, out_ref):
    experts = rows_ref.shape[0] // SLOT
    copies, count, features = out_ref.shape
    width = rows_ref.shape[1]
    quarters = features // width
    ids = jnp.concatenate([ids_ref[...]] * quarters, axis=0)
    weight = jnp.concatenate([weight_ref[...]] * quarters, axis=0)
    tokens, top = ids.shape
    mask = slot_mask(ids, experts)
    lane = lax.broadcasted_iota(jnp.int32, (tokens, experts), 1)
    rest = jnp.zeros((tokens, experts), jnp.float32)
    for j in range(top):
        rest = rest + jnp.where(ids[:, j:j + 1] == lane, weight[:, j:j + 1], 0.0)
    spread = expand(experts)
    total = None
    for _ in range(3):
        part = rest.astype(jnp.bfloat16)
        rest = rest - part.astype(jnp.float32)
        wide = jnp.dot(part, spread, preferred_element_type=jnp.float32)
        wide = jnp.where(mask, wide, 0.0).astype(jnp.bfloat16)
        term = jnp.dot(wide, rows_ref[...], preferred_element_type=jnp.float32)
        total = term if total is None else total + term
    line = jnp.concatenate([total[i * count:(i + 1) * count] for i in range(quarters)], axis=1)
    line = line.astype(jnp.bfloat16)
    for i in range(copies):
        out_ref[i] = line


def combine(y, ids, weight, rows, blocks):
    count, width = ids.shape[0] // blocks, rows.shape[1]
    shape = (blocks, count, blocks * width)
    return pl.pallas_call(
        combine_kernel,
        grid_spec=pltpu.PrefetchScalarGridSpec(
            num_scalar_prefetch=1,
            grid=(1,),
            in_specs=[
                pl.BlockSpec((count, ids.shape[1]), lambda i, y: (y[0], 0)),
                pl.BlockSpec((count, ids.shape[1]), lambda i, y: (y[0], 0)),
                pl.BlockSpec(rows.shape, lambda i, y: (0, 0)),
            ],
            out_specs=pl.BlockSpec(shape, lambda i, y: (0, 0, 0)),
        ),
        out_shape=jax.ShapeDtypeStruct(shape, jnp.bfloat16),
        compiler_params=params(),
        name="combine_rows",
    )(y, ids, weight, rows)


def regroup(rows, blocks, inverse):
    line = lax.broadcasted_iota(jnp.int32, (rows, 1), 0)
    span = rows // blocks
    if inverse:
        index = (line % SLOT) // CAP * span + line // SLOT * CAP + line % CAP
    else:
        index = (line % span) // CAP * SLOT + line // span * CAP + line % CAP
    hit = lax.broadcasted_iota(jnp.int32, (rows, rows), 1) == index
    return jnp.where(hit, 1.0, 0.0).astype(jnp.bfloat16)


def gate_up_kernel(q_ref, x_ref, w0_ref, w1_ref, out_ref, held):
    @pl.when(pl.program_id(0) == 0)
    def _():
        order = regroup(x_ref.shape[0], pl.num_programs(0), False)
        moved = jnp.dot(order, x_ref[...], preferred_element_type=jnp.float32)
        held[...] = moved.astype(jnp.bfloat16)

    hidden = w0_ref.shape[3]
    x = held[...]
    for c, ref in enumerate((w0_ref, w1_ref)):
        w = jnp.concatenate([ref[0, 0], ref[0, 1]], axis=1)
        part = jnp.dot(x, w, preferred_element_type=jnp.float32)
        out_ref[:, 2 * c * hidden:2 * (c + 1) * hidden] = part.astype(jnp.bfloat16)


def gate_up(q, rows, w_own, w_other):
    slots, width = rows.shape
    blocks, _, _, hidden = w_own.shape
    wide = pl.BlockSpec((1, 2, width, hidden), lambda i, q: (i, 0, 0, 0))
    return pl.pallas_call(
        gate_up_kernel,
        grid_spec=pltpu.PrefetchScalarGridSpec(
            num_scalar_prefetch=1,
            grid=(blocks,),
            in_specs=[pl.BlockSpec((slots, width), lambda i, q: (0, 0)), wide, wide],
            out_specs=pl.BlockSpec((slots, 4 * hidden), lambda i, q: (0, q[i])),
            scratch_shapes=[pltpu.VMEM((slots, width), jnp.bfloat16)],
        ),
        out_shape=jax.ShapeDtypeStruct((slots, 4 * blocks * hidden), jnp.bfloat16),
        compiler_params=params(),
        name="gate_up",
    )(q, rows, w_own, w_other)


def down_kernel(q_ref, x_ref, w0_ref, w1_ref, out_ref, act0, act1, held):
    step = pl.program_id(0)
    parts, span, columns = x_ref.shape
    group = columns // parts
    hidden = group // 4

    @pl.when(step == 0)
    def _():
        for i in range(parts):
            start = pl.multiple_of(q_ref[i] * group, group)
            total = None
            for p in range(parts):
                term = x_ref[p, :, pl.ds(start, group)].astype(jnp.float32)
                total = term if total is None else total + term
            for c, act in enumerate((act0, act1)):
                gate = total[:, 2 * c * hidden:(2 * c + 1) * hidden]
                up = total[:, (2 * c + 1) * hidden:(2 * c + 2) * hidden]
                value = gate / (1.0 + jnp.exp(-gate)) * up
                act[:, i * hidden:(i + 1) * hidden] = value.astype(jnp.bfloat16)

    total = jnp.dot(act0[...], w0_ref[...], preferred_element_type=jnp.float32)
    total = total + jnp.dot(act1[...], w1_ref[...], preferred_element_type=jnp.float32)
    held[pl.ds(pl.multiple_of(step * span, span), span)] = total.astype(jnp.bfloat16)

    @pl.when(step == parts - 1)
    def _():
        order = regroup(parts * span, parts, True)
        moved = jnp.dot(order, held[...], preferred_element_type=jnp.float32)
        out_ref[...] = moved.astype(jnp.bfloat16)


def down(q, sums, w_own, w_other):
    parts, span, _ = sums.shape
    depth, features = w_own.shape
    width = features // parts
    part = pl.BlockSpec((depth, width), lambda i, q: (0, i))
    return pl.pallas_call(
        down_kernel,
        grid_spec=pltpu.PrefetchScalarGridSpec(
            num_scalar_prefetch=1,
            grid=(parts,),
            in_specs=[pl.BlockSpec(sums.shape, lambda i, q: (0, 0, 0)), part, part],
            out_specs=pl.BlockSpec((parts * span, width), lambda i, q: (0, 0)),
            scratch_shapes=[
                pltpu.VMEM((span, depth), jnp.bfloat16),
                pltpu.VMEM((span, depth), jnp.bfloat16),
                pltpu.VMEM((parts * span, width), jnp.bfloat16),
            ],
        ),
        out_shape=jax.ShapeDtypeStruct((parts * span, width), jnp.bfloat16),
        compiler_params=params(),
        name="down_rows",
    )(q, sums, w_own, w_other)


def shift(block, step):
    n = lax.axis_size("y")
    return lax.ppermute(block, "y", [(i, (i + step) % n) for i in range(n)])


def swap(block):
    return lax.ppermute(block, "c", [(0, 1), (1, 0)])


def swap_all(block, axis):
    return lax.all_to_all(block, axis, split_axis=0, concat_axis=0, tiled=True)


def per_device(tokens, expert_ids, route_weight, w_gate, w_up, w_down):
    ny = lax.axis_size("y")
    experts = lax.axis_size("x") * lax.axis_size("z")
    y = lax.axis_index("y").astype(jnp.int32)
    q = jnp.stack([y, (y + 3) & 3, (y + 1) & 3, (y + 2) & 3])
    width = tokens.shape[1] // ny
    half = w_down.shape[1] // 2

    sent = dispatch(q[:1], expert_ids, tokens, experts, width)
    sent, w_gate, w_up, w_down = lax.optimization_barrier((sent, w_gate, w_up, w_down))
    rows = swap_all(sent, ("x", "z"))

    def quarter(w, i):
        return lax.dynamic_slice_in_dim(w[0], q[i] * width, width, 0)

    from_before = shift(jnp.stack([quarter(w_gate, 2), quarter(w_up, 2), quarter(w_gate, 3)]), 1)
    from_after = shift(jnp.stack([quarter(w_gate, 1), quarter(w_up, 1), quarter(w_up, 3)]), -1)
    from_before, from_after, w_down = lax.optimization_barrier((from_before, from_after, w_down))
    gate_across, up_across = shift(from_before[2], 1), shift(from_after[2], -1)
    before, after = shift(w_down[0], 1), shift(w_down[0], -1)
    both_own = jnp.stack([
        quarter(w_gate, 0), quarter(w_up, 0), from_before[0], from_before[1],
        from_after[0], from_after[1], gate_across, up_across,
    ]).reshape(ny, 2, width, w_gate.shape[2])
    both_other = swap(both_own)
    across = (shift(before[:half], 1), shift(after[half:], -1))

    sums = gate_up(q, rows, both_own, both_other)
    sums, before, after, across = lax.optimization_barrier((sums, before, after, across))
    w_own = jnp.concatenate([w_down[0], before, after, *across], axis=0)
    w_other = swap(w_own)
    sums = swap_all(sums.reshape(ny, sums.shape[0] // ny, sums.shape[1]), "y")
    back = swap_all(down(q, sums, w_own, w_other), ("x", "z"))
    mine = swap_all(combine(q[:1], expert_ids, route_weight, back, ny), "y")
    return mine.reshape(tokens.shape)


def solution(mesh):
    ny = mesh.devices.shape[0]
    nz = 16
    nx = mesh.devices.shape[1] // nz // 2
    fine = Mesh(mesh.devices.reshape(ny, nx, nz, 2), ("y", "x", "z", "c"))
    ep = ("x", "z", "c")
    in_specs = (
        P(ep, None),
        P(ep, None),
        P(ep, None),
        P(ep, None, "y"),
        P(ep, None, "y"),
        P(ep, "y", None),
    )
    return jax.shard_map(
        per_device, mesh=fine, in_specs=in_specs, out_specs=P(ep, None), check_vma=False
    )
```

time: 755 us -> 204 us (0.27)
  blocking collectives: 363 us -> 40.3 us
  waiting for transfers between devices: 318 us -> 65 us
  starting transfers between devices: 11.5 us -> 69.2 us
  local copies, waits for them, and re-layouts: 39.4 us -> 14.6 us
  matrix products: 13.9 us -> 0 us
  Pallas kernels: 0 us -> 12 us
    all_to_all x1 -> x2, blocking collectives: 341 us -> 40.3 us  [swap_all(): return lax.all_to_all(block, axis, split_axis=0, concat_axis=0, tiled=True)]
    all_to_all x1 -> x2, waiting for transfers between devices: 318 us -> 49.5 us  [swap_all(): return lax.all_to_all(block, axis, split_axis=0, concat_axis=0, tiled=True)]
    ppermute x0 -> x10, starting transfers between devices: none -> 32.3 us  [the longest x8 28.4 us: shift(): return lax.ppermute(block, 'y', [(i, (i + step) % n) for i in range(n)])]
    all_to_all x1 -> x2, starting transfers between devices: 11.5 us -> 36.9 us  [swap_all(): return lax.all_to_all(block, axis, split_axis=0, concat_axis=0, tiled=True)]
    psum x1 -> x0, blocking collectives: 21.6 us -> none  [per_device(): moe_out = lax.psum(mixed_out, 'group').astype(jnp.bfloat16)]
    gather x3 -> x0, local copies, waits for them, and re-layouts: 20.6 us -> none  [the longest x1 8.89 us: combine(): flat_rows[first_index + slots].astype(jnp.float32)]
    ppermute x0 -> x10, waiting for transfers between devices: none -> 15.6 us  [the longest x8 15.5 us: shift(): return lax.ppermute(block, 'y', [(i, (i + step) % n) for i in range(n)])]
    dot_general x2 -> x0, matrix products: 13.9 us -> none  [the longest x1 11.8 us: per_device(): jnp.dot(hidden, down_local, preferred_element_type=jnp.float32)]
  transfers between devices with their start and end apart: 1 -> 12, of which waited for: 1 -> 5; matrix products, arithmetic and copies ran while one was open for 0% -> 3% of each run, Pallas kernels for 0% -> 2%
where the time goes in v1:
time: 204 us; the launch traced here: 203 us
  starting transfers between devices  69.2 us (34%)
  waiting for transfers between devices  65 us (32%)
  blocking collectives  40.3 us (20%)
  local copies, waits for them, and re-layouts  14.6 us (7%)
  Pallas kernels  12 us (6%)
    all_to_all x2, waiting for transfers between devices, swap_all(): return lax.all_to_all(block, axis, split_axis=0, concat_axis=0, tiled=True)  49.5 us
    all_to_all x2, blocking collectives, swap_all(): return lax.all_to_all(block, axis, split_axis=0, concat_axis=0, tiled=True)  40.3 us
    all_to_all x2, starting transfers between devices, swap_all(): return lax.all_to_all(block, axis, split_axis=0, concat_axis=0, tiled=True)  36.9 us
    ppermute x8, starting transfers between devices, shift(): return lax.ppermute(block, 'y', [(i, (i + step) % n) for i in range(n)])  28.4 us
    ppermute x8, waiting for transfers between devices, shift(): return lax.ppermute(block, 'y', [(i, (i + step) % n) for i in range(n)])  15.5 us
    unnamed x32, local copies, waits for them, and re-layouts  9.48 us
    pallas_call x1, Pallas kernels, down(): pl.pallas_call(down_kernel, grid_spec=pltpu.PrefetchScalarGridSpec(num_sc...  5.09 us
    pallas_call x1, Pallas kernels, gate_up(): pl.pallas_call(gate_up_kernel, grid_spec=pltpu.PrefetchScalarGridSpec(num...  4.27 us
  transfers between devices with their start and end apart: 12, of which 5 were waited for; matrix products, arithmetic and copies ran while one was open for 3% of the time, Pallas kernels for 2%

profile of v1, /device:TPU:6, one launch (start us, length us, event | category | flops | bytes accessed | tf_op | source)
XLA Modules:
  0.0 203.3 jit_solution(6473921048236923751)
XLA Ops:
  0.0 0.8 copy.8.ids_ref
  0.8 0.9 copy-done.3
  1.7 1.8 dispatch_rows.1
  3.5 1.3 constant_dynamic-slice_fusion.2
  4.8 0.1 constant_dynamic-slice_fusion.1
  4.9 0.9 pad_maximum_fusion.1
  5.8 4.9 %collective-permute-start.1 = (bf16[3,896,128]{2,1,0:T(8,128)(2,1)}, bf16[3,896,128]{2,1,0:T(8,128)(2,1)S(1)}, u32[]{:S(2)}, u32[]{:S(2)}) collective-permute-start(bf16[3,896,128]{2,1,0:T(8,128)(2,1)} %pad_maximum_fusion.1), channel_id=1, source_target_pairs={{0,384},{128,0},{256,128},{384,256},{1,385},{129,1},{257,129},{385... | collective-permute-start | bytes 2064392 | tf_op jit(solution)/shard_map/ppermute | solution.py:221
  10.8 0.9 pad_maximum_fusion
  11.7 1.9 collective-permute-start
  13.6 18.8 %all-to-all-start = ((bf16[64,8,896]{2,1,0:T(8,128)(2,1)}), bf16[64,8,896]{2,1,0:T(8,128)(2,1)S(1)}, u32[]{:S(2)}, u32[]{:S(2)}) async-start(bf16[64,8,896]{2,1,0:T(8,128)(2,1)} %bitcast.4), calls=%async_computation | async-start | bytes 1835008 | tf_op jit(solution)/shard_map/all_to_all | solution.py:229
  32.4 0.0 collective-permute-done.1
  32.4 2.5 %collective-permute-start.5 = (bf16[128,3584]{1,0:T(8,128)(2,1)}, bf16[128,3584]{1,0:T(8,128)(2,1)S(1)}, u32[]{:S(2)}, u32[]{:S(2)}) collective-permute-start(bf16[128,3584]{1,0:T(8,128)(2,1)} %bitcast.26), channel_id=1, source_target_pairs={{0,128},{128,256},{256,384},{384,0},{1,129},{129,257},{257,385},{3... | collective-permute-start | bytes 2752520 | tf_op jit(solution)/shard_map/ppermute | solution.py:221
  34.9 4.6 %collective-permute-start.6 = (bf16[128,3584]{1,0:T(8,128)(2,1)}, bf16[128,3584]{1,0:T(8,128)(2,1)S(1)}, u32[]{:S(2)}, u32[]{:S(2)}) collective-permute-start(bf16[128,3584]{1,0:T(8,128)(2,1)} %bitcast.27), channel_id=1, source_target_pairs={{0,384},{128,0},{256,128},{384,256},{1,385},{129,1},{257,129},{385... | collective-permute-start | bytes 2752520 | tf_op jit(solution)/shard_map/ppermute | solution.py:221
  39.5 1.0 slice_bitcast_fusion.1
  40.5 1.9 collective-permute-start.2
  42.4 5.1 %collective-permute-start.3 = (bf16[896,128]{1,0:T(8,128)(2,1)S(1)}, bf16[896,128]{1,0:T(8,128)(2,1)S(1)}, u32[]{:S(2)}, u32[]{:S(2)}) collective-permute-start(bf16[896,128]{1,0:T(8,128)(2,1)S(1)} %slice_bitcast_fusion), channel_id=1, source_target_pairs={{0,384},{128,0},{256,128},{384,256},{1,385},{129,1},{257,129},{385... | collective-permute-start | bytes 688136 | tf_op jit(solution)/shard_map/ppermute | solution.py:221
  47.6 1.1 slice_dynamic-update-slice_fusion.1
  48.6 0.0 copy-start.8
  48.7 0.1 slice_dynamic-update-slice_fusion
  48.7 13.2 %collective-permute-done.2 = bf16[896,128]{1,0:T(8,128)(2,1)S(1)} collective-permute-done((bf16[896,128]{1,0:T(8,128)(2,1)S(1)}, bf16[896,128]{1,0:T(8,128)(2,1)S(1)}, u32[]{:S(2)}, u32[]{:S(2)}) %collective-permute-start.2) | collective-permute-done | bytes 229408 | tf_op jit(solution)/shard_map/ppermute | solution.py:221
  62.0 1.1 collective-permute-done.3
  63.1 1.9 collective-permute-start.4
  65.1 0.1 pad_add_fusion.q_ref
  65.1 0.9 copy-done.4
  66.1 0.8 slice.28
  66.9 3.8 %collective-permute-start.7 = (bf16[64,3584]{1,0:T(8,128)(2,1)}, bf16[64,3584]{1,0:T(8,128)(2,1)S(1)}, u32[]{:S(2)}, u32[]{:S(2)}) collective-permute-start(bf16[64,3584]{1,0:T(8,128)(2,1)} %slice.28), channel_id=1, source_target_pairs={{0,128},{128,256},{256,384},{384,0},{1,129},{129,257},{257,385},{3... | collective-permute-start | bytes 1376264 | tf_op jit(solution)/shard_map/ppermute | solution.py:221
  70.7 1.0 copy-done.6
  71.7 0.8 slice.29
  72.5 3.7 %collective-permute-start.8 = (bf16[64,3584]{1,0:T(8,128)(2,1)}, bf16[64,3584]{1,0:T(8,128)(2,1)}, u32[]{:S(2)}, u32[]{:S(2)}) collective-permute-start(bf16[64,3584]{1,0:T(8,128)(2,1)} %slice.29), channel_id=1, source_target_pairs={{0,384},{128,0},{256,128},{384,256},{1,385},{129,1},{257,129},{385... | collective-permute-start | bytes 1376264 | tf_op jit(solution)/shard_map/ppermute | solution.py:221
  76.2 1.0 constant_dynamic-update-slice_fusion.4
  77.3 1.3 copy-done.1
  78.5 1.8 all-to-all-done
  80.3 1.5 copy-done.2
  81.8 4.3 %gate_up.1 = bf16[512,2048]{1,0:T(8,128)(2,1)S(1)} custom-call(s32[4]{0:T(128)S(1)} %pad_add_fusion.q_ref, bf16[512,896]{1,0:T(8,128)(2,1)S(1)} %bitcast.23, bf16[4,2,896,128]{3,2,1,0:T(8,128)(2,1)S(1)} %bitcast.25, bf16[4,2,896,128]{3,2,1,0:T(8,128)(2,1)S(1)} %copy-done.2), custom_call_target="tpu_custom_call" | custom-call | tf_op jit(solution)/shard_map/gate_up/pallas_call | solution.py:149
  86.1 1.2 collective-permute-done.8
  87.3 0.1 constant_dynamic-update-slice_fusion.3
  87.4 0.1 constant_dynamic-update-slice_fusion.2
  87.5 1.1 constant_dynamic-update-slice_fusion.w0_ref
  88.6 1.9 collective-permute-start.9
  90.5 31.4 %all_to_all.32.x_ref = bf16[4,128,2048]{2,1,0:T(8,128)(2,1)S(1)} all-to-all(bf16[4,128,2048]{2,1,0:T(8,128)(2,1)S(1)} %bitcast.21), channel_id=1, replica_groups=mesh['y'=4,'x'=4,'z'=16,'c'=2] {'y'}, dimensions={0} | all-to-all | bytes 4194304 | tf_op jit(solution)/shard_map/all_to_all | solution.py:229
  121.9 0.0 collective-permute-done.9.w1_ref
  121.9 5.1 %down_rows.1 = bf16[512,896]{1,0:T(8,128)(2,1)} custom-call(s32[4]{0:T(128)S(1)} %pad_add_fusion.q_ref, bf16[4,128,2048]{2,1,0:T(8,128)(2,1)S(1)} %all_to_all.32.x_ref, bf16[512,3584]{1,0:T(8,128)(2,1)S(1)} %constant_dynamic-update-slice_fusion.w0_ref, bf16[512,3584]{1,0:T(8,128)(2,1)S(1)} %collective-permute-done.9.w1_ref), custom_call_target="tpu_custom_call" | custom-call | tf_op jit(solution)/shard_map/down_rows/pallas_call | solution.py:200
  127.0 18.1 %all-to-all-start.2 = ((bf16[64,8,896]{2,1,0:T(8,128)(2,1)}), bf16[64,8,896]{2,1,0:T(8,128)(2,1)S(1)}, u32[]{:S(2)}, u32[]{:S(2)}) async-start(bf16[64,8,896]{2,1,0:T(8,128)(2,1)} %bitcast.13), calls=%async_computation.2 | async-start | bytes 1835008 | tf_op jit(solution)/shard_map/all_to_all | solution.py:229
  145.1 0.1 copy.9.weight_ref
  145.2 47.6 %all-to-all-done.2 = bf16[64,8,896]{2,1,0:T(8,128)(2,1)S(1)} async-done(((bf16[64,8,896]{2,1,0:T(8,128)(2,1)}), bf16[64,8,896]{2,1,0:T(8,128)(2,1)S(1)}, u32[]{:S(2)}, u32[]{:S(2)}) %all-to-all-start.2) | async-done | bytes 917536 | tf_op jit(solution)/shard_map/all_to_all | solution.py:229
  192.8 0.9 combine_rows.1
  193.7 8.9 %all_to_all.33 = bf16[4,8,3584]{2,1,0:T(8,128)(2,1)S(1)} all-to-all(bf16[4,8,3584]{2,1,0:T(8,128)(2,1)S(1)} %combine_rows.1), channel_id=1, replica_groups=mesh['y'=4,'x'=4,'z'=16,'c'=2] {'y'}, dimensions={0} | all-to-all | bytes 458752 | tf_op jit(solution)/shard_map/all_to_all | solution.py:229
  202.6 0.7 copy.20
  (25 shorter events, 0.2 us)
Async XLA Ops:
  0.8 0.9 copy-start.3
  1.7 3.1 %copy-start.9 = (bf16[1,3584,128]{2,1,0:T(8,128)(2,1)S(1)}, bf16[1,3584,128]{2,1,0:T(8,128)(2,1)}, u32[]{:S(2)}) copy-start(bf16[1,3584,128]{2,1,0:T(8,128)(2,1)} %param.10) | copy-start | bytes 2752516
  5.8 26.6 %collective-permute-start.1 = (bf16[3,896,128]{2,1,0:T(8,128)(2,1)}, bf16[3,896,128]{2,1,0:T(8,128)(2,1)S(1)}, u32[]{:S(2)}, u32[]{:S(2)}) collective-permute-start(bf16[3,896,128]{2,1,0:T(8,128)(2,1)} %pad_maximum_fusion.1), channel_id=1, source_target_pairs={{0,384},{128,0},{256,128},{384,256},{1,385},{129,1},{257,129},{385... | collective-permute-start | bytes 2064392 | tf_op jit(solution)/shard_map/ppermute | solution.py:221
  11.7 20.7 %collective-permute-start = (bf16[3,896,128]{2,1,0:T(8,128)(2,1)}, bf16[3,896,128]{2,1,0:T(8,128)(2,1)}, u32[]{:S(2)}, u32[]{:S(2)}) collective-permute-start(bf16[3,896,128]{2,1,0:T(8,128)(2,1)} %pad_maximum_fusion), channel_id=1, source_target_pairs={{0,128},{128,256},{256,384},{384,0},{1,129},{129,257},{257,385},{3... | collective-permute-start | bytes 2064392 | tf_op jit(solution)/shard_map/ppermute | solution.py:221
  13.6 66.7 %all-to-all-start = ((bf16[64,8,896]{2,1,0:T(8,128)(2,1)}), bf16[64,8,896]{2,1,0:T(8,128)(2,1)S(1)}, u32[]{:S(2)}, u32[]{:S(2)}) async-start(bf16[64,8,896]{2,1,0:T(8,128)(2,1)} %bitcast.4), calls=%async_computation | async-start | bytes 1835008 | tf_op jit(solution)/shard_map/all_to_all | solution.py:229
  32.4 32.7 %collective-permute-start.5 = (bf16[128,3584]{1,0:T(8,128)(2,1)}, bf16[128,3584]{1,0:T(8,128)(2,1)S(1)}, u32[]{:S(2)}, u32[]{:S(2)}) collective-permute-start(bf16[128,3584]{1,0:T(8,128)(2,1)} %bitcast.26), channel_id=1, source_target_pairs={{0,128},{128,256},{256,384},{384,0},{1,129},{129,257},{257,385},{3... | collective-permute-start | bytes 2752520 | tf_op jit(solution)/shard_map/ppermute | solution.py:221
  34.9 35.8 %collective-permute-start.6 = (bf16[128,3584]{1,0:T(8,128)(2,1)}, bf16[128,3584]{1,0:T(8,128)(2,1)S(1)}, u32[]{:S(2)}, u32[]{:S(2)}) collective-permute-start(bf16[128,3584]{1,0:T(8,128)(2,1)} %bitcast.27), channel_id=1, source_target_pairs={{0,384},{128,0},{256,128},{384,256},{1,385},{129,1},{257,129},{385... | collective-permute-start | bytes 2752520 | tf_op jit(solution)/shard_map/ppermute | solution.py:221
  40.5 21.5 %collective-permute-start.2 = (bf16[896,128]{1,0:T(8,128)(2,1)S(1)}, bf16[896,128]{1,0:T(8,128)(2,1)S(1)}, u32[]{:S(2)}, u32[]{:S(2)}) collective-permute-start(bf16[896,128]{1,0:T(8,128)(2,1)S(1)} %slice_bitcast_fusion.1), channel_id=1, source_target_pairs={{0,128},{128,256},{256,384},{384,0},{1,129},{129,257},{257,385},{3... | collective-permute-start | bytes 688136 | tf_op jit(solution)/shard_map/ppermute | solution.py:221
  42.4 20.7 %collective-permute-start.3 = (bf16[896,128]{1,0:T(8,128)(2,1)S(1)}, bf16[896,128]{1,0:T(8,128)(2,1)S(1)}, u32[]{:S(2)}, u32[]{:S(2)}) collective-permute-start(bf16[896,128]{1,0:T(8,128)(2,1)S(1)} %slice_bitcast_fusion), channel_id=1, source_target_pairs={{0,384},{128,0},{256,128},{384,256},{1,385},{129,1},{257,129},{385... | collective-permute-start | bytes 688136 | tf_op jit(solution)/shard_map/ppermute | solution.py:221
  48.6 27.6 %copy-start.8 = (bf16[1,128,3584]{2,1,0:T(8,128)(2,1)S(1)}, bf16[1,128,3584]{2,1,0:T(8,128)(2,1)}, u32[]{:S(2)}) copy-start(bf16[1,128,3584]{2,1,0:T(8,128)(2,1)} %param.11) | copy-start | bytes 2752516
  63.1 14.1 %collective-permute-start.4 = (bf16[4,2,896,128]{3,2,1,0:T(8,128)(2,1)S(1)}, bf16[4,2,896,128]{3,2,1,0:T(8,128)(2,1)S(1)}, u32[]{:S(2)}, u32[]{:S(2)}) collective-permute-start(bf16[4,2,896,128]{3,2,1,0:T(8,128)(2,1)S(1)} %bitcast.24), channel_id=1, source_target_pairs={{0,1},{1,0},{2,3},{3,2},{4,5},{5,4},{6,7},{7,6},{8,9},{9,8},{10,11... | collective-permute-start | bytes 5505032 | tf_op jit(solution)/shard_map/ppermute | solution.py:225
  65.1 0.9 copy-start.4
  66.9 19.2 %collective-permute-start.7 = (bf16[64,3584]{1,0:T(8,128)(2,1)}, bf16[64,3584]{1,0:T(8,128)(2,1)S(1)}, u32[]{:S(2)}, u32[]{:S(2)}) collective-permute-start(bf16[64,3584]{1,0:T(8,128)(2,1)} %slice.28), channel_id=1, source_target_pairs={{0,128},{128,256},{256,384},{384,0},{1,129},{129,257},{257,385},{3... | collective-permute-start | bytes 1376264 | tf_op jit(solution)/shard_map/ppermute | solution.py:221
  70.7 1.0 copy-start.6
  72.5 14.8 %collective-permute-start.8 = (bf16[64,3584]{1,0:T(8,128)(2,1)}, bf16[64,3584]{1,0:T(8,128)(2,1)}, u32[]{:S(2)}, u32[]{:S(2)}) collective-permute-start(bf16[64,3584]{1,0:T(8,128)(2,1)} %slice.29), channel_id=1, source_target_pairs={{0,384},{128,0},{256,128},{384,256},{1,385},{129,1},{257,129},{385... | collective-permute-start | bytes 1376264 | tf_op jit(solution)/shard_map/ppermute | solution.py:221
  77.2 1.3 copy-start.1
  80.3 1.5 copy-start.2
  81.8 5.5 %copy-start = (bf16[512,3584]{1,0:T(8,128)(2,1)S(1)}, bf16[512,3584]{1,0:T(8,128)(2,1)}, u32[]{:S(2)}) copy-start(bf16[512,3584]{1,0:T(8,128)(2,1)} %constant_dynamic-update-slice_fusion.4) | copy-start | bytes 11010052
  81.8 5.5 %copy-start.5 = (bf16[128,3584]{1,0:T(8,128)(2,1)S(1)}, bf16[128,3584]{1,0:T(8,128)(2,1)}, u32[]{:S(2)}) copy-start(bf16[128,3584]{1,0:T(8,128)(2,1)} %copy-done.4) | copy-start | bytes 2752516
  86.1 1.3 copy-start.7
  88.6 33.3 %collective-permute-start.9 = (bf16[512,3584]{1,0:T(8,128)(2,1)S(1)}, bf16[512,3584]{1,0:T(8,128)(2,1)S(1)}, u32[]{:S(2)}, u32[]{:S(2)}) collective-permute-start(bf16[512,3584]{1,0:T(8,128)(2,1)S(1)} %constant_dynamic-update-slice_fusion.w0_ref), channel_id=1, source_target_pairs={{0,1},{1,0},{2,3},{3,2},{4,5},{5,4},{6,7},{7,6},{8,9},{9,8},{10,11... | collective-permute-start | bytes 11010056 | tf_op jit(solution)/shard_map/ppermute | solution.py:225
  127.0 18.1 %copy-start.10 = (f32[32,8]{0,1:T(8,128)S(1)}, f32[32,8]{0,1:T(8,128)}, u32[]{:S(2)}) copy-start(f32[32,8]{0,1:T(8,128)} %param.8) | copy-start | bytes 3076
  127.0 65.8 %all-to-all-start.2 = ((bf16[64,8,896]{2,1,0:T(8,128)(2,1)}), bf16[64,8,896]{2,1,0:T(8,128)(2,1)S(1)}, u32[]{:S(2)}, u32[]{:S(2)}) async-start(bf16[64,8,896]{2,1,0:T(8,128)(2,1)} %bitcast.13), calls=%async_computation.2 | async-start | bytes 1835008 | tf_op jit(solution)/shard_map/all_to_all | solution.py:229

commit v2 on v1

--- a/solution.py
+++ b/solution.py
@@ -41,7 +41,15 @@
 
 def dispatch_kernel(y_ref, ids_ref, tokens_ref, out_ref):
     experts = out_ref.shape[0] // SLOT
-    onehot = jnp.where(slot_mask(ids_ref[...], experts), 1.0, 0.0).astype(jnp.bfloat16)
+    count = tokens_ref.shape[0]
+    row = lax.broadcasted_iota(jnp.int32, (count, count), 0)
+    col = lax.broadcasted_iota(jnp.int32, (count, count), 1)
+    unit = jnp.where(row == col, 1.0, 0.0).astype(jnp.bfloat16)
+    across = ids_ref[...].astype(jnp.float32).astype(jnp.bfloat16)
+    ids = lax.dot_general(
+        unit, across, (((1,), (1,)), ((), ())), preferred_element_type=jnp.float32
+    ).astype(jnp.int32)
+    onehot = jnp.where(slot_mask(ids, experts), 1.0, 0.0).astype(jnp.bfloat16)
     rows = lax.dot_general(
         onehot, tokens_ref[...], (((0,), (0,)), ((), ())), preferred_element_type=jnp.float32
     )
@@ -229,6 +237,29 @@
     return lax.all_to_all(block, axis, split_axis=0, concat_axis=0, tiled=True)
 
 
+def cut_kernel(q_ref, *refs):
+    gates, ups, outs = refs[0:4], refs[4:8], refs[8:12]
+    for gate, up, out in zip(gates, ups, outs):
+        out[0] = gate[...]
+        out[1] = up[...]
+
+
+def cut(q, gate, up):
+    depth, hidden = gate.shape
+    width = depth // 4
+    parts = [pl.BlockSpec((width, hidden), lambda s, q, i=i: (q[i], 0)) for i in range(4)]
+    whole = pl.BlockSpec((2, width, hidden), lambda s, q: (0, 0, 0))
+    return pl.pallas_call(
+        cut_kernel,
+        grid_spec=pltpu.PrefetchScalarGridSpec(
+            num_scalar_prefetch=1, grid=(1,), in_specs=parts + parts, out_specs=[whole] * 4
+        ),
+        out_shape=[jax.ShapeDtypeStruct((2, width, hidden), gate.dtype)] * 4,
+        compiler_params=params(),
+        name="cut_quarters",
+    )(q, *[gate] * 4, *[up] * 4)
+
+
 def per_device(tokens, expert_ids, route_weight, w_gate, w_up, w_down):
     ny = lax.axis_size("y")
     experts = lax.axis_size("x") * lax.axis_size("z")
@@ -237,28 +268,22 @@
     width = tokens.shape[1] // ny
     half = w_down.shape[1] // 2
 
-    sent = dispatch(q[:1], expert_ids, tokens, experts, width)
+    sent = dispatch(q[:1], expert_ids.T, tokens, experts, width)
     sent, w_gate, w_up, w_down = lax.optimization_barrier((sent, w_gate, w_up, w_down))
     rows = swap_all(sent, ("x", "z"))
 
-    def quarter(w, i):
-        return lax.dynamic_slice_in_dim(w[0], q[i] * width, width, 0)
-
-    from_before = shift(jnp.stack([quarter(w_gate, 2), quarter(w_up, 2), quarter(w_gate, 3)]), 1)
-    from_after = shift(jnp.stack([quarter(w_gate, 1), quarter(w_up, 1), quarter(w_up, 3)]), -1)
-    from_before, from_after, w_down = lax.optimization_barrier((from_before, from_after, w_down))
-    gate_across, up_across = shift(from_before[2], 1), shift(from_after[2], -1)
+    own, prior, later, across = cut(q, w_gate[0], w_up[0])
+    pieces = [own, shift(later, 1), shift(prior, -1), shift(across, 2)]
+    *pieces, w_down = lax.optimization_barrier((*pieces, w_down))
+    both_own = jnp.stack(pieces)
+    both_other = swap(both_own)
+
     before, after = shift(w_down[0], 1), shift(w_down[0], -1)
-    both_own = jnp.stack([
-        quarter(w_gate, 0), quarter(w_up, 0), from_before[0], from_before[1],
-        from_after[0], from_after[1], gate_across, up_across,
-    ]).reshape(ny, 2, width, w_gate.shape[2])
-    both_other = swap(both_own)
-    across = (shift(before[:half], 1), shift(after[half:], -1))
+    relayed = (shift(before[:half], 1), shift(after[half:], -1))
 
     sums = gate_up(q, rows, both_own, both_other)
-    sums, before, after, across = lax.optimization_barrier((sums, before, after, across))
-    w_own = jnp.concatenate([w_down[0], before, after, *across], axis=0)
+    sums, before, after, relayed = lax.optimization_barrier((sums, before, after, relayed))
+    w_own = jnp.concatenate([w_down[0], before, after, *relayed], axis=0)
     w_other = swap(w_own)
     sums = swap_all(sums.reshape(ny, sums.shape[0] // ny, sums.shape[1]), "y")
     back = swap_all(down(q, sums, w_own, w_other), ("x", "z"))

time: 204 us -> 205 us (level)
  waiting for transfers between devices: 65 us -> 76.8 us
  starting transfers between devices: 69.2 us -> 63.3 us
  local copies, waits for them, and re-layouts: 14.6 us -> 11.7 us
    ppermute x8 -> x7, waiting for transfers between devices: 15.5 us -> 29.2 us  [shift(): return lax.ppermute(block, 'y', [(i, (i + step) % n) for i in range(n)])]
    all_to_all x2, starting transfers between devices: 36.9 us -> 33.9 us  [swap_all(): return lax.all_to_all(block, axis, split_axis=0, concat_axis=0, tiled=True)]
    ppermute x8 -> x7, starting transfers between devices: 28.4 us -> 25.5 us  [shift(): return lax.ppermute(block, 'y', [(i, (i + step) % n) for i in range(n)])]
    unnamed x32 -> x35, local copies, waits for them, and re-layouts: 9.48 us -> 8.9 us
  transfers between devices with their start and end apart: 12 -> 11, of which waited for: 5 -> 5; matrix products, arithmetic and copies ran while one was open for 3% -> 2% of each run, Pallas kernels for 2% -> 2%
where the time goes in v2:
time: 205 us
  waiting for transfers between devices  76.8 us (37%)
  starting transfers between devices  63.3 us (31%)
  blocking collectives  39.5 us (19%)
  Pallas kernels  12.8 us (6%)
  local copies, waits for them, and re-layouts  11.7 us (6%)
    all_to_all x2, waiting for transfers between devices, swap_all(): return lax.all_to_all(block, axis, split_axis=0, concat_axis=0, tiled=True)  47.6 us
    all_to_all x2, blocking collectives, swap_all(): return lax.all_to_all(block, axis, split_axis=0, concat_axis=0, tiled=True)  39.5 us
    all_to_all x2, starting transfers between devices, swap_all(): return lax.all_to_all(block, axis, split_axis=0, concat_axis=0, tiled=True)  33.9 us
    ppermute x7, waiting for transfers between devices, shift(): return lax.ppermute(block, 'y', [(i, (i + step) % n) for i in range(n)])  29.2 us
    ppermute x7, starting transfers between devices, shift(): return lax.ppermute(block, 'y', [(i, (i + step) % n) for i in range(n)])  25.5 us
    unnamed x35, local copies, waits for them, and re-layouts  8.9 us
    pallas_call x1, Pallas kernels, down(): pl.pallas_call(down_kernel, grid_spec=pltpu.PrefetchScalarGridSpec(num_sc...  5.09 us
    pallas_call x1, Pallas kernels, gate_up(): pl.pallas_call(gate_up_kernel, grid_spec=pltpu.PrefetchScalarGridSpec(num...  4.31 us
  transfers between devices with their start and end apart: 11, of which 5 were waited for; matrix products, arithmetic and copies ran while one was open for 2% of the time, Pallas kernels for 2%

profile of v2, /device:TPU:6, one launch (start us, length us, event | category | flops | bytes accessed | tf_op | source)
XLA Modules:
  0.0 204.6 jit_solution(2779590425431605554)
XLA Ops:
  0.0 0.9 copy-done.5
  0.9 0.7 copy-done.6
  1.6 1.9 dispatch_rows.1
  3.5 18.8 %all-to-all-start = ((bf16[64,8,896]{2,1,0:T(8,128)(2,1)}), bf16[64,8,896]{2,1,0:T(8,128)(2,1)S(1)}, u32[]{:S(2)}, u32[]{:S(2)}) async-start(bf16[64,8,896]{2,1,0:T(8,128)(2,1)} %bitcast.5), calls=%async_computation | async-start | bytes 1835008 | tf_op jit(solution)/shard_map/all_to_all | solution.py:237
  22.3 0.1 pad_add_fusion.q_ref
  22.4 1.2 copy-done
  23.5 1.2 copy-done.1
  24.7 0.7 cut_quarters.1
  25.4 3.5 %collective-permute-start = (bf16[2,896,128]{2,1,0:T(8,128)(2,1)S(1)}, bf16[2,896,128]{2,1,0:T(8,128)(2,1)S(1)}, u32[]{:S(2)}, u32[]{:S(2)}) collective-permute-start(bf16[2,896,128]{2,1,0:T(8,128)(2,1)S(1)} %get-tuple-element.27), channel_id=1, source_target_pairs={{0,128},{128,256},{256,384},{384,0},{1,129},{129,257},{257,385},{3... | collective-permute-start | bytes 1376264 | tf_op jit(solution)/shard_map/ppermute | solution.py:229
  28.9 3.6 %collective-permute-start.1 = (bf16[2,896,128]{2,1,0:T(8,128)(2,1)S(1)}, bf16[2,896,128]{2,1,0:T(8,128)(2,1)S(1)}, u32[]{:S(2)}, u32[]{:S(2)}) collective-permute-start(bf16[2,896,128]{2,1,0:T(8,128)(2,1)S(1)} %get-tuple-element.28), channel_id=1, source_target_pairs={{0,384},{128,0},{256,128},{384,256},{1,385},{129,1},{257,129},{385... | collective-permute-start | bytes 1376264 | tf_op jit(solution)/shard_map/ppermute | solution.py:229
  32.5 3.9 %collective-permute-start.2 = (bf16[2,896,128]{2,1,0:T(8,128)(2,1)S(1)}, bf16[2,896,128]{2,1,0:T(8,128)(2,1)S(1)}, u32[]{:S(2)}, u32[]{:S(2)}) collective-permute-start(bf16[2,896,128]{2,1,0:T(8,128)(2,1)S(1)} %get-tuple-element.29), channel_id=1, source_target_pairs={{0,256},{128,384},{256,0},{384,128},{1,257},{129,385},{257,1},{385... | collective-permute-start | bytes 1376264 | tf_op jit(solution)/shard_map/ppermute | solution.py:229
  36.4 4.5 %collective-permute-done = bf16[2,896,128]{2,1,0:T(8,128)(2,1)S(1)} collective-permute-done((bf16[2,896,128]{2,1,0:T(8,128)(2,1)S(1)}, bf16[2,896,128]{2,1,0:T(8,128)(2,1)S(1)}, u32[]{:S(2)}, u32[]{:S(2)}) %collective-permute-start) | collective-permute-done | bytes 458784 | tf_op jit(solution)/shard_map/ppermute | solution.py:229
  40.9 3.4 %collective-permute-done.1 = bf16[2,896,128]{2,1,0:T(8,128)(2,1)S(1)} collective-permute-done((bf16[2,896,128]{2,1,0:T(8,128)(2,1)S(1)}, bf16[2,896,128]{2,1,0:T(8,128)(2,1)S(1)}, u32[]{:S(2)}, u32[]{:S(2)}) %collective-permute-start.1) | collective-permute-done | bytes 458784 | tf_op jit(solution)/shard_map/ppermute | solution.py:229
  44.2 7.0 %collective-permute-done.2 = bf16[2,896,128]{2,1,0:T(8,128)(2,1)S(1)} collective-permute-done((bf16[2,896,128]{2,1,0:T(8,128)(2,1)S(1)}, bf16[2,896,128]{2,1,0:T(8,128)(2,1)S(1)}, u32[]{:S(2)}, u32[]{:S(2)}) %collective-permute-start.2) | collective-permute-done | bytes 458784 | tf_op jit(solution)/shard_map/ppermute | solution.py:229
  51.3 5.0 %collective-permute-start.4 = (bf16[128,3584]{1,0:T(8,128)(2,1)S(1)}, bf16[128,3584]{1,0:T(8,128)(2,1)S(1)}, u32[]{:S(2)}, u32[]{:S(2)}) collective-permute-start(bf16[128,3584]{1,0:T(8,128)(2,1)S(1)} %bitcast.32), channel_id=1, source_target_pairs={{0,128},{128,256},{256,384},{384,0},{1,129},{129,257},{257,385},{3... | collective-permute-start | bytes 2752520 | tf_op jit(solution)/shard_map/ppermute | solution.py:229
  56.2 2.6 %collective-permute-start.5 = (bf16[128,3584]{1,0:T(8,128)(2,1)S(1)}, bf16[128,3584]{1,0:T(8,128)(2,1)S(1)}, u32[]{:S(2)}, u32[]{:S(2)}) collective-permute-start(bf16[128,3584]{1,0:T(8,128)(2,1)S(1)} %bitcast.33), channel_id=1, source_target_pairs={{0,384},{128,0},{256,128},{384,256},{1,385},{129,1},{257,129},{385... | collective-permute-start | bytes 2752520 | tf_op jit(solution)/shard_map/ppermute | solution.py:229
  58.8 0.2 pad_maximum_fusion.w0_ref
  59.1 1.9 collective-permute-start.3
  61.0 14.2 %collective-permute-done.4 = bf16[128,3584]{1,0:T(8,128)(2,1)S(1)} collective-permute-done((bf16[128,3584]{1,0:T(8,128)(2,1)S(1)}, bf16[128,3584]{1,0:T(8,128)(2,1)S(1)}, u32[]{:S(2)}, u32[]{:S(2)}) %collective-permute-start.4) | collective-permute-done | bytes 917536 | tf_op jit(solution)/shard_map/ppermute | solution.py:229
  75.2 0.9 slice.8
  76.2 3.2 %collective-permute-start.6 = (bf16[64,3584]{1,0:T(8,128)(2,1)}, bf16[64,3584]{1,0:T(8,128)(2,1)S(1)}, u32[]{:S(2)}, u32[]{:S(2)}) collective-permute-start(bf16[64,3584]{1,0:T(8,128)(2,1)} %slice.8), channel_id=1, source_target_pairs={{0,128},{128,256},{256,384},{384,0},{1,129},{129,257},{257,385},{3... | collective-permute-start | bytes 1376264 | tf_op jit(solution)/shard_map/ppermute | solution.py:229
  79.4 0.0 collective-permute-done.5
  79.4 0.0 copy-start.10
  79.4 0.8 slice.9
  80.2 3.8 %collective-permute-start.7 = (bf16[64,3584]{1,0:T(8,128)(2,1)}, bf16[64,3584]{1,0:T(8,128)(2,1)}, u32[]{:S(2)}, u32[]{:S(2)}) collective-permute-start(bf16[64,3584]{1,0:T(8,128)(2,1)} %slice.9), channel_id=1, source_target_pairs={{0,384},{128,0},{256,128},{384,256},{1,385},{129,1},{257,129},{385... | collective-permute-start | bytes 1376264 | tf_op jit(solution)/shard_map/ppermute | solution.py:229
  84.1 1.0 constant_dynamic-update-slice_fusion.4
  85.1 0.0 copy-done.8
  85.1 0.0 collective-permute-done.3.w1_ref
  85.1 1.2 copy-done.3
  86.3 0.0 all-to-all-done
  86.3 1.6 copy-done.4
  88.0 4.3 %gate_up.1 = bf16[512,2048]{1,0:T(8,128)(2,1)S(1)} custom-call(s32[4]{0:T(128)S(1)} %pad_add_fusion.q_ref, bf16[512,896]{1,0:T(8,128)(2,1)S(1)} %bitcast.29, bf16[4,2,896,128]{3,2,1,0:T(8,128)(2,1)S(1)} %pad_maximum_fusion.w0_ref, bf16[4,2,896,128]{3,2,1,0:T(8,128)(2,1)S(1)} %copy-done.4), custom_call_target="tpu_custom_call" | custom-call | tf_op jit(solution)/shard_map/gate_up/pallas_call | solution.py:157
  92.3 0.0 collective-permute-done.6
  92.3 0.0 collective-permute-done.7
  92.4 0.1 constant_dynamic-update-slice_fusion.3
  92.4 0.1 constant_dynamic-update-slice_fusion.2
  92.5 1.1 constant_dynamic-update-slice_fusion.w0_ref
  93.6 1.9 collective-permute-start.8
  95.5 30.6 %all_to_all.32.x_ref = bf16[4,128,2048]{2,1,0:T(8,128)(2,1)S(1)} all-to-all(bf16[4,128,2048]{2,1,0:T(8,128)(2,1)S(1)} %bitcast.27), channel_id=1, replica_groups=mesh['y'=4,'x'=4,'z'=16,'c'=2] {'y'}, dimensions={0} | all-to-all | bytes 4194304 | tf_op jit(solution)/shard_map/all_to_all | solution.py:237
  126.2 0.0 collective-permute-done.8.w1_ref
  126.2 5.1 %down_rows.1 = bf16[512,896]{1,0:T(8,128)(2,1)} custom-call(s32[4]{0:T(128)S(1)} %pad_add_fusion.q_ref, bf16[4,128,2048]{2,1,0:T(8,128)(2,1)S(1)} %all_to_all.32.x_ref, bf16[512,3584]{1,0:T(8,128)(2,1)S(1)} %constant_dynamic-update-slice_fusion.w0_ref, bf16[512,3584]{1,0:T(8,128)(2,1)S(1)} %collective-permute-done.8.w1_ref), custom_call_target="tpu_custom_call" | custom-call | tf_op jit(solution)/shard_map/down_rows/pallas_call | solution.py:208
  131.3 15.1 %all-to-all-start.2 = ((bf16[64,8,896]{2,1,0:T(8,128)(2,1)}), bf16[64,8,896]{2,1,0:T(8,128)(2,1)S(1)}, u32[]{:S(2)}, u32[]{:S(2)}) async-start(bf16[64,8,896]{2,1,0:T(8,128)(2,1)} %bitcast.15), calls=%async_computation.2 | async-start | bytes 1835008 | tf_op jit(solution)/shard_map/all_to_all | solution.py:237
  146.4 0.1 copy.7.ids_ref
  146.5 0.1 copy.8.weight_ref
  146.6 47.6 %all-to-all-done.2 = bf16[64,8,896]{2,1,0:T(8,128)(2,1)S(1)} async-done(((bf16[64,8,896]{2,1,0:T(8,128)(2,1)}), bf16[64,8,896]{2,1,0:T(8,128)(2,1)S(1)}, u32[]{:S(2)}, u32[]{:S(2)}) %all-to-all-start.2) | async-done | bytes 917536 | tf_op jit(solution)/shard_map/all_to_all | solution.py:237
  194.1 0.9 combine_rows.1
  195.1 8.9 %all_to_all.33 = bf16[4,8,3584]{2,1,0:T(8,128)(2,1)S(1)} all-to-all(bf16[4,8,3584]{2,1,0:T(8,128)(2,1)S(1)} %combine_rows.1), channel_id=1, replica_groups=mesh['y'=4,'x'=4,'z'=16,'c'=2] {'y'}, dimensions={0} | all-to-all | bytes 458752 | tf_op jit(solution)/shard_map/all_to_all | solution.py:237
  203.9 0.7 copy.14
  (21 shorter events, 0.1 us)
Async XLA Ops:
  0.0 0.9 copy-start.5
  0.9 0.7 copy-start.6
  3.5 82.9 %all-to-all-start = ((bf16[64,8,896]{2,1,0:T(8,128)(2,1)}), bf16[64,8,896]{2,1,0:T(8,128)(2,1)S(1)}, u32[]{:S(2)}, u32[]{:S(2)}) async-start(bf16[64,8,896]{2,1,0:T(8,128)(2,1)} %bitcast.5), calls=%async_computation | async-start | bytes 1835008 | tf_op jit(solution)/shard_map/all_to_all | solution.py:237
  22.4 1.2 copy-start
  23.5 1.2 copy-start.1
  24.7 26.6 %copy-start.12 = (bf16[1,128,3584]{2,1,0:T(8,128)(2,1)S(1)}, bf16[1,128,3584]{2,1,0:T(8,128)(2,1)}, u32[]{:S(2)}) copy-start(bf16[1,128,3584]{2,1,0:T(8,128)(2,1)} %param.11) | copy-start | bytes 2752516
  25.4 15.5 %collective-permute-start = (bf16[2,896,128]{2,1,0:T(8,128)(2,1)S(1)}, bf16[2,896,128]{2,1,0:T(8,128)(2,1)S(1)}, u32[]{:S(2)}, u32[]{:S(2)}) collective-permute-start(bf16[2,896,128]{2,1,0:T(8,128)(2,1)S(1)} %get-tuple-element.27), channel_id=1, source_target_pairs={{0,128},{128,256},{256,384},{384,0},{1,129},{129,257},{257,385},{3... | collective-permute-start | bytes 1376264 | tf_op jit(solution)/shard_map/ppermute | solution.py:229
  28.9 15.4 %collective-permute-start.1 = (bf16[2,896,128]{2,1,0:T(8,128)(2,1)S(1)}, bf16[2,896,128]{2,1,0:T(8,128)(2,1)S(1)}, u32[]{:S(2)}, u32[]{:S(2)}) collective-permute-start(bf16[2,896,128]{2,1,0:T(8,128)(2,1)S(1)} %get-tuple-element.28), channel_id=1, source_target_pairs={{0,384},{128,0},{256,128},{384,256},{1,385},{129,1},{257,129},{385... | collective-permute-start | bytes 1376264 | tf_op jit(solution)/shard_map/ppermute | solution.py:229
  32.5 18.8 %collective-permute-start.2 = (bf16[2,896,128]{2,1,0:T(8,128)(2,1)S(1)}, bf16[2,896,128]{2,1,0:T(8,128)(2,1)S(1)}, u32[]{:S(2)}, u32[]{:S(2)}) collective-permute-start(bf16[2,896,128]{2,1,0:T(8,128)(2,1)S(1)} %get-tuple-element.29), channel_id=1, source_target_pairs={{0,256},{128,384},{256,0},{384,128},{1,257},{129,385},{257,1},{385... | collective-permute-start | bytes 1376264 | tf_op jit(solution)/shard_map/ppermute | solution.py:229
  51.3 24.0 %collective-permute-start.4 = (bf16[128,3584]{1,0:T(8,128)(2,1)S(1)}, bf16[128,3584]{1,0:T(8,128)(2,1)S(1)}, u32[]{:S(2)}, u32[]{:S(2)}) collective-permute-start(bf16[128,3584]{1,0:T(8,128)(2,1)S(1)} %bitcast.32), channel_id=1, source_target_pairs={{0,128},{128,256},{256,384},{384,0},{1,129},{129,257},{257,385},{3... | collective-permute-start | bytes 2752520 | tf_op jit(solution)/shard_map/ppermute | solution.py:229
  56.2 23.1 %collective-permute-start.5 = (bf16[128,3584]{1,0:T(8,128)(2,1)S(1)}, bf16[128,3584]{1,0:T(8,128)(2,1)S(1)}, u32[]{:S(2)}, u32[]{:S(2)}) collective-permute-start(bf16[128,3584]{1,0:T(8,128)(2,1)S(1)} %bitcast.33), channel_id=1, source_target_pairs={{0,384},{128,0},{256,128},{384,256},{1,385},{129,1},{257,129},{385... | collective-permute-start | bytes 2752520 | tf_op jit(solution)/shard_map/ppermute | solution.py:229
  59.1 26.0 %collective-permute-start.3 = (bf16[4,2,896,128]{3,2,1,0:T(8,128)(2,1)S(1)}, bf16[4,2,896,128]{3,2,1,0:T(8,128)(2,1)S(1)}, u32[]{:S(2)}, u32[]{:S(2)}) collective-permute-start(bf16[4,2,896,128]{3,2,1,0:T(8,128)(2,1)S(1)} %pad_maximum_fusion.w0_ref), channel_id=1, source_target_pairs={{0,1},{1,0},{2,3},{3,2},{4,5},{5,4},{6,7},{7,6},{8,9},{9,8},{10,11... | collective-permute-start | bytes 5505032 | tf_op jit(solution)/shard_map/ppermute | solution.py:233
  75.2 9.8 %copy-start.8 = (bf16[128,3584]{1,0:T(8,128)(2,1)}, bf16[128,3584]{1,0:T(8,128)(2,1)S(1)}, u32[]{:S(2)}) copy-start(bf16[128,3584]{1,0:T(8,128)(2,1)S(1)} %collective-permute-done.4) | copy-start | bytes 2752516
  76.2 16.2 %collective-permute-start.6 = (bf16[64,3584]{1,0:T(8,128)(2,1)}, bf16[64,3584]{1,0:T(8,128)(2,1)S(1)}, u32[]{:S(2)}, u32[]{:S(2)}) collective-permute-start(bf16[64,3584]{1,0:T(8,128)(2,1)} %slice.8), channel_id=1, source_target_pairs={{0,128},{128,256},{256,384},{384,0},{1,129},{129,257},{257,385},{3... | collective-permute-start | bytes 1376264 | tf_op jit(solution)/shard_map/ppermute | solution.py:229
  79.4 5.7 %copy-start.10 = (bf16[128,3584]{1,0:T(8,128)(2,1)}, bf16[128,3584]{1,0:T(8,128)(2,1)S(1)}, u32[]{:S(2)}) copy-start(bf16[128,3584]{1,0:T(8,128)(2,1)S(1)} %collective-permute-done.5) | copy-start | bytes 2752516
  80.2 12.1 %collective-permute-start.7 = (bf16[64,3584]{1,0:T(8,128)(2,1)}, bf16[64,3584]{1,0:T(8,128)(2,1)}, u32[]{:S(2)}, u32[]{:S(2)}) collective-permute-start(bf16[64,3584]{1,0:T(8,128)(2,1)} %slice.9), channel_id=1, source_target_pairs={{0,384},{128,0},{256,128},{384,256},{1,385},{129,1},{257,129},{385... | collective-permute-start | bytes 1376264 | tf_op jit(solution)/shard_map/ppermute | solution.py:229
  85.1 1.2 copy-start.3
  86.3 6.0 %copy-start.2 = (bf16[512,3584]{1,0:T(8,128)(2,1)S(1)}, bf16[512,3584]{1,0:T(8,128)(2,1)}, u32[]{:S(2)}) copy-start(bf16[512,3584]{1,0:T(8,128)(2,1)} %constant_dynamic-update-slice_fusion.4) | copy-start | bytes 11010052
  86.3 1.7 copy-start.4
  88.0 4.4 %copy-start.9 = (bf16[128,3584]{1,0:T(8,128)(2,1)S(1)}, bf16[128,3584]{1,0:T(8,128)(2,1)}, u32[]{:S(2)}) copy-start(bf16[128,3584]{1,0:T(8,128)(2,1)} %copy-done.8) | copy-start | bytes 2752516
  88.0 4.4 %copy-start.11 = (bf16[128,3584]{1,0:T(8,128)(2,1)S(1)}, bf16[128,3584]{1,0:T(8,128)(2,1)}, u32[]{:S(2)}) copy-start(bf16[128,3584]{1,0:T(8,128)(2,1)} %copy-done.10) | copy-start | bytes 2752516
  93.6 32.6 %collective-permute-start.8 = (bf16[512,3584]{1,0:T(8,128)(2,1)S(1)}, bf16[512,3584]{1,0:T(8,128)(2,1)S(1)}, u32[]{:S(2)}, u32[]{:S(2)}) collective-permute-start(bf16[512,3584]{1,0:T(8,128)(2,1)S(1)} %constant_dynamic-update-slice_fusion.w0_ref), channel_id=1, source_target_pairs={{0,1},{1,0},{2,3},{3,2},{4,5},{5,4},{6,7},{7,6},{8,9},{9,8},{10,11... | collective-permute-start | bytes 11010056 | tf_op jit(solution)/shard_map/ppermute | solution.py:233
  126.2 20.2 %copy-start.7 = (s32[32,8]{0,1:T(8,128)S(1)}, s32[32,8]{0,1:T(8,128)}, u32[]{:S(2)}) copy-start(s32[32,8]{0,1:T(8,128)} %param.7) | copy-start | bytes 3076
  126.2 20.3 %copy-start.13 = (f32[32,8]{0,1:T(8,128)S(1)}, f32[32,8]{0,1:T(8,128)}, u32[]{:S(2)}) copy-start(f32[32,8]{0,1:T(8,128)} %param.8) | copy-start | bytes 3076
  131.3 62.9 %all-to-all-start.2 = ((bf16[64,8,896]{2,1,0:T(8,128)(2,1)}), bf16[64,8,896]{2,1,0:T(8,128)(2,1)S(1)}, u32[]{:S(2)}, u32[]{:S(2)}) async-start(bf16[64,8,896]{2,1,0:T(8,128)(2,1)} %bitcast.15), calls=%async_computation.2 | async-start | bytes 1835008 | tf_op jit(solution)/shard_map/all_to_all | solution.py:237

commit v3 on v2

--- a/solution.py
+++ b/solution.py
@@ -272,9 +272,9 @@
     sent, w_gate, w_up, w_down = lax.optimization_barrier((sent, w_gate, w_up, w_down))
     rows = swap_all(sent, ("x", "z"))
 
-    own, prior, later, across = cut(q, w_gate[0], w_up[0])
+    cuts = cut(q, w_gate[0], w_up[0])
+    own, prior, later, across, w_down = lax.optimization_barrier((*cuts, w_down))
     pieces = [own, shift(later, 1), shift(prior, -1), shift(across, 2)]
-    *pieces, w_down = lax.optimization_barrier((*pieces, w_down))
     both_own = jnp.stack(pieces)
     both_other = swap(both_own)
 

time: 205 us -> 202 us (0.985)
  waiting for transfers between devices: 76.8 us -> 72.4 us
    ppermute x7, waiting for transfers between devices: 29.2 us -> 24.8 us  [shift(): return lax.ppermute(block, 'y', [(i, (i + step) % n) for i in range(n)])]
where the time goes in v3:
time: 202 us; the launch traced here: 201 us
  waiting for transfers between devices  72.4 us (36%)
  starting transfers between devices  62.8 us (31%)
  blocking collectives  40.6 us (20%)
  Pallas kernels  12.8 us (6%)
  local copies, waits for them, and re-layouts  11.7 us (6%)
    all_to_all x2, waiting for transfers between devices, swap_all(): return lax.all_to_all(block, axis, split_axis=0, concat_axis=0, tiled=True)  47.5 us
    all_to_all x2, blocking collectives, swap_all(): return lax.all_to_all(block, axis, split_axis=0, concat_axis=0, tiled=True)  40.6 us
    all_to_all x2, starting transfers between devices, swap_all(): return lax.all_to_all(block, axis, split_axis=0, concat_axis=0, tiled=True)  33.9 us
    ppermute x7, starting transfers between devices, shift(): return lax.ppermute(block, 'y', [(i, (i + step) % n) for i in range(n)])  25 us
    ppermute x7, waiting for transfers between devices, shift(): return lax.ppermute(block, 'y', [(i, (i + step) % n) for i in range(n)])  24.8 us
    unnamed x35, local copies, waits for them, and re-layouts  8.9 us
    pallas_call x1, Pallas kernels, down(): pl.pallas_call(down_kernel, grid_spec=pltpu.PrefetchScalarGridSpec(num_sc...  5.09 us
    pallas_call x1, Pallas kernels, gate_up(): pl.pallas_call(gate_up_kernel, grid_spec=pltpu.PrefetchScalarGridSpec(num...  4.3 us
  transfers between devices with their start and end apart: 11, of which 5 were waited for; matrix products, arithmetic and copies ran while one was open for 2% of the time, Pallas kernels for 2%

profile of v3, /device:TPU:6, one launch (start us, length us, event | category | flops | bytes accessed | tf_op | source)
XLA Modules:
  0.0 200.9 jit_solution(3341097900943399248)
XLA Ops:
  0.0 0.9 copy-done.5
  0.9 0.7 copy-done.6
  1.6 1.9 dispatch_rows.1
  3.5 18.8 %all-to-all-start = ((bf16[64,8,896]{2,1,0:T(8,128)(2,1)}), bf16[64,8,896]{2,1,0:T(8,128)(2,1)S(1)}, u32[]{:S(2)}, u32[]{:S(2)}) async-start(bf16[64,8,896]{2,1,0:T(8,128)(2,1)} %bitcast.5), calls=%async_computation | async-start | bytes 1835008 | tf_op jit(solution)/shard_map/all_to_all | solution.py:237
  22.3 0.1 pad_add_fusion.q_ref
  22.4 1.2 copy-done
  23.5 1.2 copy-done.1
  24.7 0.7 cut_quarters.1
  25.4 3.5 %collective-permute-start = (bf16[2,896,128]{2,1,0:T(8,128)(2,1)S(1)}, bf16[2,896,128]{2,1,0:T(8,128)(2,1)S(1)}, u32[]{:S(2)}, u32[]{:S(2)}) collective-permute-start(bf16[2,896,128]{2,1,0:T(8,128)(2,1)S(1)} %get-tuple-element.32), channel_id=1, source_target_pairs={{0,128},{128,256},{256,384},{384,0},{1,129},{129,257},{257,385},{3... | collective-permute-start | bytes 1376264 | tf_op jit(solution)/shard_map/ppermute | solution.py:229
  28.9 3.6 %collective-permute-start.1 = (bf16[2,896,128]{2,1,0:T(8,128)(2,1)S(1)}, bf16[2,896,128]{2,1,0:T(8,128)(2,1)S(1)}, u32[]{:S(2)}, u32[]{:S(2)}) collective-permute-start(bf16[2,896,128]{2,1,0:T(8,128)(2,1)S(1)} %get-tuple-element.33), channel_id=1, source_target_pairs={{0,384},{128,0},{256,128},{384,256},{1,385},{129,1},{257,129},{385... | collective-permute-start | bytes 1376264 | tf_op jit(solution)/shard_map/ppermute | solution.py:229
  32.5 3.9 %collective-permute-start.2 = (bf16[2,896,128]{2,1,0:T(8,128)(2,1)S(1)}, bf16[2,896,128]{2,1,0:T(8,128)(2,1)S(1)}, u32[]{:S(2)}, u32[]{:S(2)}) collective-permute-start(bf16[2,896,128]{2,1,0:T(8,128)(2,1)S(1)} %get-tuple-element.34), channel_id=1, source_target_pairs={{0,256},{128,384},{256,0},{384,128},{1,257},{129,385},{257,1},{385... | collective-permute-start | bytes 1376264 | tf_op jit(solution)/shard_map/ppermute | solution.py:229
  36.4 0.0 copy-done.12
  36.4 2.6 %collective-permute-start.4 = (bf16[128,3584]{1,0:T(8,128)(2,1)S(1)}, bf16[128,3584]{1,0:T(8,128)(2,1)S(1)}, u32[]{:S(2)}, u32[]{:S(2)}) collective-permute-start(bf16[128,3584]{1,0:T(8,128)(2,1)S(1)} %bitcast.32), channel_id=1, source_target_pairs={{0,128},{128,256},{256,384},{384,0},{1,129},{129,257},{257,385},{3... | collective-permute-start | bytes 2752520 | tf_op jit(solution)/shard_map/ppermute | solution.py:229
  39.0 4.5 %collective-permute-start.5 = (bf16[128,3584]{1,0:T(8,128)(2,1)S(1)}, bf16[128,3584]{1,0:T(8,128)(2,1)S(1)}, u32[]{:S(2)}, u32[]{:S(2)}) collective-permute-start(bf16[128,3584]{1,0:T(8,128)(2,1)S(1)} %bitcast.33), channel_id=1, source_target_pairs={{0,384},{128,0},{256,128},{384,256},{1,385},{129,1},{257,129},{385... | collective-permute-start | bytes 2752520 | tf_op jit(solution)/shard_map/ppermute | solution.py:229
  43.4 0.0 collective-permute-done
  43.5 7.4 %collective-permute-done.1 = bf16[2,896,128]{2,1,0:T(8,128)(2,1)S(1)} collective-permute-done((bf16[2,896,128]{2,1,0:T(8,128)(2,1)S(1)}, bf16[2,896,128]{2,1,0:T(8,128)(2,1)S(1)}, u32[]{:S(2)}, u32[]{:S(2)}) %collective-permute-start.1) | collective-permute-done | bytes 458784 | tf_op jit(solution)/shard_map/ppermute | solution.py:229
  50.9 2.2 %collective-permute-done.2 = bf16[2,896,128]{2,1,0:T(8,128)(2,1)S(1)} collective-permute-done((bf16[2,896,128]{2,1,0:T(8,128)(2,1)S(1)}, bf16[2,896,128]{2,1,0:T(8,128)(2,1)S(1)}, u32[]{:S(2)}, u32[]{:S(2)}) %collective-permute-start.2) | collective-permute-done | bytes 458784 | tf_op jit(solution)/shard_map/ppermute | solution.py:229
  53.1 0.2 pad_maximum_fusion.w0_ref
  53.3 1.9 collective-permute-start.3
  55.2 14.5 %collective-permute-done.4 = bf16[128,3584]{1,0:T(8,128)(2,1)S(1)} collective-permute-done((bf16[128,3584]{1,0:T(8,128)(2,1)S(1)}, bf16[128,3584]{1,0:T(8,128)(2,1)S(1)}, u32[]{:S(2)}, u32[]{:S(2)}) %collective-permute-start.4) | collective-permute-done | bytes 917536 | tf_op jit(solution)/shard_map/ppermute | solution.py:229
  69.8 0.9 slice.8
  70.7 2.2 %collective-permute-start.6 = (bf16[64,3584]{1,0:T(8,128)(2,1)}, bf16[64,3584]{1,0:T(8,128)(2,1)S(1)}, u32[]{:S(2)}, u32[]{:S(2)}) collective-permute-start(bf16[64,3584]{1,0:T(8,128)(2,1)} %slice.8), channel_id=1, source_target_pairs={{0,128},{128,256},{256,384},{384,0},{1,129},{129,257},{257,385},{3... | collective-permute-start | bytes 1376264 | tf_op jit(solution)/shard_map/ppermute | solution.py:229
  72.9 0.0 collective-permute-done.5
  72.9 0.0 copy-start.10
  73.0 0.8 slice.9
  73.8 4.8 %collective-permute-start.7 = (bf16[64,3584]{1,0:T(8,128)(2,1)}, bf16[64,3584]{1,0:T(8,128)(2,1)}, u32[]{:S(2)}, u32[]{:S(2)}) collective-permute-start(bf16[64,3584]{1,0:T(8,128)(2,1)} %slice.9), channel_id=1, source_target_pairs={{0,384},{128,0},{256,128},{384,256},{1,385},{129,1},{257,129},{385... | collective-permute-start | bytes 1376264 | tf_op jit(solution)/shard_map/ppermute | solution.py:229
  78.6 1.0 constant_dynamic-update-slice_fusion.4
  79.6 0.0 collective-permute-done.3.w1_ref
  79.6 1.2 copy-done.3
  80.9 0.0 all-to-all-done
  80.9 1.6 copy-done.4
  82.5 4.3 %gate_up.1 = bf16[512,2048]{1,0:T(8,128)(2,1)S(1)} custom-call(s32[4]{0:T(128)S(1)} %pad_add_fusion.q_ref, bf16[512,896]{1,0:T(8,128)(2,1)S(1)} %bitcast.29, bf16[4,2,896,128]{3,2,1,0:T(8,128)(2,1)S(1)} %pad_maximum_fusion.w0_ref, bf16[4,2,896,128]{3,2,1,0:T(8,128)(2,1)S(1)} %copy-done.4), custom_call_target="tpu_custom_call" | custom-call | tf_op jit(solution)/shard_map/gate_up/pallas_call | solution.py:157
  86.8 0.0 collective-permute-done.6
  86.8 0.7 collective-permute-done.7
  87.5 0.1 constant_dynamic-update-slice_fusion.3
  87.6 0.1 constant_dynamic-update-slice_fusion.2
  87.7 1.1 constant_dynamic-update-slice_fusion.w0_ref
  88.8 1.9 collective-permute-start.8
  90.7 31.8 %all_to_all.32.x_ref = bf16[4,128,2048]{2,1,0:T(8,128)(2,1)S(1)} all-to-all(bf16[4,128,2048]{2,1,0:T(8,128)(2,1)S(1)} %bitcast.27), channel_id=1, replica_groups=mesh['y'=4,'x'=4,'z'=16,'c'=2] {'y'}, dimensions={0} | all-to-all | bytes 4194304 | tf_op jit(solution)/shard_map/all_to_all | solution.py:237
  122.4 0.0 collective-permute-done.8.w1_ref
  122.5 5.1 %down_rows.1 = bf16[512,896]{1,0:T(8,128)(2,1)} custom-call(s32[4]{0:T(128)S(1)} %pad_add_fusion.q_ref, bf16[4,128,2048]{2,1,0:T(8,128)(2,1)S(1)} %all_to_all.32.x_ref, bf16[512,3584]{1,0:T(8,128)(2,1)S(1)} %constant_dynamic-update-slice_fusion.w0_ref, bf16[512,3584]{1,0:T(8,128)(2,1)S(1)} %collective-permute-done.8.w1_ref), custom_call_target="tpu_custom_call" | custom-call | tf_op jit(solution)/shard_map/down_rows/pallas_call | solution.py:208
  127.5 15.1 %all-to-all-start.2 = ((bf16[64,8,896]{2,1,0:T(8,128)(2,1)}), bf16[64,8,896]{2,1,0:T(8,128)(2,1)S(1)}, u32[]{:S(2)}, u32[]{:S(2)}) async-start(bf16[64,8,896]{2,1,0:T(8,128)(2,1)} %bitcast.15), calls=%async_computation.2 | async-start | bytes 1835008 | tf_op jit(solution)/shard_map/all_to_all | solution.py:237
  142.7 0.1 copy.7.ids_ref
  142.8 0.1 copy.8.weight_ref
  142.8 47.5 %all-to-all-done.2 = bf16[64,8,896]{2,1,0:T(8,128)(2,1)S(1)} async-done(((bf16[64,8,896]{2,1,0:T(8,128)(2,1)}), bf16[64,8,896]{2,1,0:T(8,128)(2,1)S(1)}, u32[]{:S(2)}, u32[]{:S(2)}) %all-to-all-start.2) | async-done | bytes 917536 | tf_op jit(solution)/shard_map/all_to_all | solution.py:237
  190.4 0.9 combine_rows.1
  191.3 8.9 %all_to_all.33 = bf16[4,8,3584]{2,1,0:T(8,128)(2,1)S(1)} all-to-all(bf16[4,8,3584]{2,1,0:T(8,128)(2,1)S(1)} %combine_rows.1), channel_id=1, replica_groups=mesh['y'=4,'x'=4,'z'=16,'c'=2] {'y'}, dimensions={0} | all-to-all | bytes 458752 | tf_op jit(solution)/shard_map/all_to_all | solution.py:237
  200.2 0.7 copy.14
  (21 shorter events, 0.1 us)
Async XLA Ops:
  0.0 0.9 copy-start.5
  0.9 0.7 copy-start.6
  3.5 77.4 %all-to-all-start = ((bf16[64,8,896]{2,1,0:T(8,128)(2,1)}), bf16[64,8,896]{2,1,0:T(8,128)(2,1)S(1)}, u32[]{:S(2)}, u32[]{:S(2)}) async-start(bf16[64,8,896]{2,1,0:T(8,128)(2,1)} %bitcast.5), calls=%async_computation | async-start | bytes 1835008 | tf_op jit(solution)/shard_map/all_to_all | solution.py:237
  22.4 1.2 copy-start
  23.5 1.2 copy-start.1
  24.7 11.6 %copy-start.12 = (bf16[1,128,3584]{2,1,0:T(8,128)(2,1)S(1)}, bf16[1,128,3584]{2,1,0:T(8,128)(2,1)}, u32[]{:S(2)}) copy-start(bf16[1,128,3584]{2,1,0:T(8,128)(2,1)} %param.11) | copy-start | bytes 2752516
  25.4 18.1 %collective-permute-start = (bf16[2,896,128]{2,1,0:T(8,128)(2,1)S(1)}, bf16[2,896,128]{2,1,0:T(8,128)(2,1)S(1)}, u32[]{:S(2)}, u32[]{:S(2)}) collective-permute-start(bf16[2,896,128]{2,1,0:T(8,128)(2,1)S(1)} %get-tuple-element.32), channel_id=1, source_target_pairs={{0,128},{128,256},{256,384},{384,0},{1,129},{129,257},{257,385},{3... | collective-permute-start | bytes 1376264 | tf_op jit(solution)/shard_map/ppermute | solution.py:229
  28.9 22.0 %collective-permute-start.1 = (bf16[2,896,128]{2,1,0:T(8,128)(2,1)S(1)}, bf16[2,896,128]{2,1,0:T(8,128)(2,1)S(1)}, u32[]{:S(2)}, u32[]{:S(2)}) collective-permute-start(bf16[2,896,128]{2,1,0:T(8,128)(2,1)S(1)} %get-tuple-element.33), channel_id=1, source_target_pairs={{0,384},{128,0},{256,128},{384,256},{1,385},{129,1},{257,129},{385... | collective-permute-start | bytes 1376264 | tf_op jit(solution)/shard_map/ppermute | solution.py:229
  32.5 20.6 %collective-permute-start.2 = (bf16[2,896,128]{2,1,0:T(8,128)(2,1)S(1)}, bf16[2,896,128]{2,1,0:T(8,128)(2,1)S(1)}, u32[]{:S(2)}, u32[]{:S(2)}) collective-permute-start(bf16[2,896,128]{2,1,0:T(8,128)(2,1)S(1)} %get-tuple-element.34), channel_id=1, source_target_pairs={{0,256},{128,384},{256,0},{384,128},{1,257},{129,385},{257,1},{385... | collective-permute-start | bytes 1376264 | tf_op jit(solution)/shard_map/ppermute | solution.py:229
  36.4 33.4 %collective-permute-start.4 = (bf16[128,3584]{1,0:T(8,128)(2,1)S(1)}, bf16[128,3584]{1,0:T(8,128)(2,1)S(1)}, u32[]{:S(2)}, u32[]{:S(2)}) collective-permute-start(bf16[128,3584]{1,0:T(8,128)(2,1)S(1)} %bitcast.32), channel_id=1, source_target_pairs={{0,128},{128,256},{256,384},{384,0},{1,129},{129,257},{257,385},{3... | collective-permute-start | bytes 2752520 | tf_op jit(solution)/shard_map/ppermute | solution.py:229
  39.0 34.0 %collective-permute-start.5 = (bf16[128,3584]{1,0:T(8,128)(2,1)S(1)}, bf16[128,3584]{1,0:T(8,128)(2,1)S(1)}, u32[]{:S(2)}, u32[]{:S(2)}) collective-permute-start(bf16[128,3584]{1,0:T(8,128)(2,1)S(1)} %bitcast.33), channel_id=1, source_target_pairs={{0,384},{128,0},{256,128},{384,256},{1,385},{129,1},{257,129},{385... | collective-permute-start | bytes 2752520 | tf_op jit(solution)/shard_map/ppermute | solution.py:229
  53.3 26.3 %collective-permute-start.3 = (bf16[4,2,896,128]{3,2,1,0:T(8,128)(2,1)S(1)}, bf16[4,2,896,128]{3,2,1,0:T(8,128)(2,1)S(1)}, u32[]{:S(2)}, u32[]{:S(2)}) collective-permute-start(bf16[4,2,896,128]{3,2,1,0:T(8,128)(2,1)S(1)} %pad_maximum_fusion.w0_ref), channel_id=1, source_target_pairs={{0,1},{1,0},{2,3},{3,2},{4,5},{5,4},{6,7},{7,6},{8,9},{9,8},{10,11... | collective-permute-start | bytes 5505032 | tf_op jit(solution)/shard_map/ppermute | solution.py:233
  69.8 9.8 %copy-start.8 = (bf16[128,3584]{1,0:T(8,128)(2,1)}, bf16[128,3584]{1,0:T(8,128)(2,1)S(1)}, u32[]{:S(2)}) copy-start(bf16[128,3584]{1,0:T(8,128)(2,1)S(1)} %collective-permute-done.4) | copy-start | bytes 2752516
  70.7 16.1 %collective-permute-start.6 = (bf16[64,3584]{1,0:T(8,128)(2,1)}, bf16[64,3584]{1,0:T(8,128)(2,1)S(1)}, u32[]{:S(2)}, u32[]{:S(2)}) collective-permute-start(bf16[64,3584]{1,0:T(8,128)(2,1)} %slice.8), channel_id=1, source_target_pairs={{0,128},{128,256},{256,384},{384,0},{1,129},{129,257},{257,385},{3... | collective-permute-start | bytes 1376264 | tf_op jit(solution)/shard_map/ppermute | solution.py:229
  72.9 6.7 %copy-start.10 = (bf16[128,3584]{1,0:T(8,128)(2,1)}, bf16[128,3584]{1,0:T(8,128)(2,1)S(1)}, u32[]{:S(2)}) copy-start(bf16[128,3584]{1,0:T(8,128)(2,1)S(1)} %collective-permute-done.5) | copy-start | bytes 2752516
  73.8 13.7 %collective-permute-start.7 = (bf16[64,3584]{1,0:T(8,128)(2,1)}, bf16[64,3584]{1,0:T(8,128)(2,1)}, u32[]{:S(2)}, u32[]{:S(2)}) collective-permute-start(bf16[64,3584]{1,0:T(8,128)(2,1)} %slice.9), channel_id=1, source_target_pairs={{0,384},{128,0},{256,128},{384,256},{1,385},{129,1},{257,129},{385... | collective-permute-start | bytes 1376264 | tf_op jit(solution)/shard_map/ppermute | solution.py:229
  79.6 1.2 copy-start.3
  80.9 6.7 %copy-start.2 = (bf16[512,3584]{1,0:T(8,128)(2,1)S(1)}, bf16[512,3584]{1,0:T(8,128)(2,1)}, u32[]{:S(2)}) copy-start(bf16[512,3584]{1,0:T(8,128)(2,1)} %constant_dynamic-update-slice_fusion.4) | copy-start | bytes 11010052
  80.9 1.7 copy-start.4
  82.5 5.0 %copy-start.9 = (bf16[128,3584]{1,0:T(8,128)(2,1)S(1)}, bf16[128,3584]{1,0:T(8,128)(2,1)}, u32[]{:S(2)}) copy-start(bf16[128,3584]{1,0:T(8,128)(2,1)} %copy-done.8) | copy-start | bytes 2752516
  82.5 5.1 %copy-start.11 = (bf16[128,3584]{1,0:T(8,128)(2,1)S(1)}, bf16[128,3584]{1,0:T(8,128)(2,1)}, u32[]{:S(2)}) copy-start(bf16[128,3584]{1,0:T(8,128)(2,1)} %copy-done.10) | copy-start | bytes 2752516
  88.8 33.7 %collective-permute-start.8 = (bf16[512,3584]{1,0:T(8,128)(2,1)S(1)}, bf16[512,3584]{1,0:T(8,128)(2,1)S(1)}, u32[]{:S(2)}, u32[]{:S(2)}) collective-permute-start(bf16[512,3584]{1,0:T(8,128)(2,1)S(1)} %constant_dynamic-update-slice_fusion.w0_ref), channel_id=1, source_target_pairs={{0,1},{1,0},{2,3},{3,2},{4,5},{5,4},{6,7},{7,6},{8,9},{9,8},{10,11... | collective-permute-start | bytes 11010056 | tf_op jit(solution)/shard_map/ppermute | solution.py:233
  122.4 20.2 %copy-start.7 = (s32[32,8]{0,1:T(8,128)S(1)}, s32[32,8]{0,1:T(8,128)}, u32[]{:S(2)}) copy-start(s32[32,8]{0,1:T(8,128)} %param.7) | copy-start | bytes 3076
  122.4 20.3 %copy-start.13 = (f32[32,8]{0,1:T(8,128)S(1)}, f32[32,8]{0,1:T(8,128)}, u32[]{:S(2)}) copy-start(f32[32,8]{0,1:T(8,128)} %param.8) | copy-start | bytes 3076
  127.5 62.8 %all-to-all-start.2 = ((bf16[64,8,896]{2,1,0:T(8,128)(2,1)}), bf16[64,8,896]{2,1,0:T(8,128)(2,1)S(1)}, u32[]{:S(2)}, u32[]{:S(2)}) async-start(bf16[64,8,896]{2,1,0:T(8,128)(2,1)} %bitcast.15), calls=%async_computation.2 | async-start | bytes 1835008 | tf_op jit(solution)/shard_map/all_to_all | solution.py:237

commit v4 on v3

--- a/solution.py
+++ b/solution.py
@@ -11,8 +11,8 @@
 MIB = 1 << 20
 
 
-def params():
-    return pltpu.CompilerParams(vmem_limit_bytes=24 * MIB)
+def params(limit=24):
+    return pltpu.CompilerParams(vmem_limit_bytes=limit * MIB)
 
 
 def slot_mask(ids, experts):
@@ -70,7 +70,7 @@
             out_specs=pl.BlockSpec((experts * SLOT, width), lambda i, y: (0, 0)),
         ),
         out_shape=jax.ShapeDtypeStruct((experts * SLOT, width), tokens.dtype),
-        compiler_params=params(),
+        compiler_params=params(60),
         name="dispatch_rows",
     )(y, ids, tokens)
 
@@ -255,7 +255,7 @@
             num_scalar_prefetch=1, grid=(1,), in_specs=parts + parts, out_specs=[whole] * 4
         ),
         out_shape=[jax.ShapeDtypeStruct((2, width, hidden), gate.dtype)] * 4,
-        compiler_params=params(),
+        compiler_params=params(60),
         name="cut_quarters",
     )(q, *[gate] * 4, *[up] * 4)
 

time: 202 us -> 202 us (level)
  Pallas kernels: 12.8 us -> 16.5 us
  local copies, waits for them, and re-layouts: 11.7 us -> 8.91 us
    pallas_call x1, Pallas kernels: 0.66 us -> 3.5 us  [cut(): pl.pallas_call(cut_kernel, grid_spec=pltpu.PrefetchScalarGridSpec(num_sca...]
    unnamed x35 -> x27, local copies, waits for them, and re-layouts: 8.9 us -> 6.1 us
  transfers between devices with their start and end apart: 11 -> 11, of which waited for: 5 -> 4; matrix products, arithmetic and copies ran while one was open for 2% -> 3% of each run, Pallas kernels for 2% -> 4%
where the time goes in v4:
time: 202 us; the launch traced here: 201 us
  waiting for transfers between devices  70.9 us (35%)
  starting transfers between devices  62.8 us (31%)
  blocking collectives  40.1 us (20%)
  Pallas kernels  16.5 us (8%)
  local copies, waits for them, and re-layouts  8.91 us (4%)
    all_to_all x2, waiting for transfers between devices, swap_all(): return lax.all_to_all(block, axis, split_axis=0, concat_axis=0, tiled=True)  47.5 us
    all_to_all x2, blocking collectives, swap_all(): return lax.all_to_all(block, axis, split_axis=0, concat_axis=0, tiled=True)  40.1 us
    all_to_all x2, starting transfers between devices, swap_all(): return lax.all_to_all(block, axis, split_axis=0, concat_axis=0, tiled=True)  33.9 us
    ppermute x7, starting transfers between devices, shift(): return lax.ppermute(block, 'y', [(i, (i + step) % n) for i in range(n)])  25 us
    ppermute x7, waiting for transfers between devices, shift(): return lax.ppermute(block, 'y', [(i, (i + step) % n) for i in range(n)])  23.4 us
    unnamed x27, local copies, waits for them, and re-layouts  6.1 us
    pallas_call x1, Pallas kernels, down(): pl.pallas_call(down_kernel, grid_spec=pltpu.PrefetchScalarGridSpec(num_sc...  5.09 us
    pallas_call x1, Pallas kernels, gate_up(): pl.pallas_call(gate_up_kernel, grid_spec=pltpu.PrefetchScalarGridSpec(num...  4.28 us
  transfers between devices with their start and end apart: 11, of which 4 were waited for; matrix products, arithmetic and copies ran while one was open for 3% of the time, Pallas kernels for 4%

profile of v4, /device:TPU:6, one launch (start us, length us, event | category | flops | bytes accessed | tf_op | source)
XLA Modules:
  0.0 201.3 jit_solution(16480674814766138344)
XLA Ops:
  0.0 2.7 %dispatch_rows.1 = bf16[512,896]{1,0:T(8,128)(2,1)} custom-call(s32[1]{0:T(128)} %bitcast.y_ref, s32[8,32]{1,0:T(8,128)} %bitcast.36, bf16[32,3584]{1,0:T(8,128)(2,1)} %tokens_ref.1), custom_call_target="tpu_custom_call" | custom-call | tf_op jit(solution)/shard_map/dispatch_rows/pallas_call | solution.py:61
  2.7 18.8 %all-to-all-start = ((bf16[64,8,896]{2,1,0:T(8,128)(2,1)}), bf16[64,8,896]{2,1,0:T(8,128)(2,1)S(1)}, u32[]{:S(2)}, u32[]{:S(2)}) async-start(bf16[64,8,896]{2,1,0:T(8,128)(2,1)} %bitcast.30), calls=%async_computation | async-start | bytes 1835008 | tf_op jit(solution)/shard_map/all_to_all | solution.py:237
  21.5 0.7 pad_add_fusion.q_ref
  22.2 3.5 %cut_quarters.1 = (bf16[2,896,128]{2,1,0:T(8,128)(2,1)}, bf16[2,896,128]{2,1,0:T(8,128)(2,1)}, bf16[2,896,128]{2,1,0:T(8,128)(2,1)}, bf16[2,896,128]{2,1,0:T(8,128)(2,1)}) custom-call(s32[4]{0:T(128)} %pad_add_fusion.q_ref, bf16[3584,128]{1,0:T(8,128)(2,1)} %bitcast.22, bf16[3584,128]{1,0:T(8,128)(2,1)} %bitcast.23, bf16[3584,128]{1,0:T(8,128)(2,1)} %bitcast.24, ...), custom_call_target="tpu_custom_call" | custom-call | tf_op jit(solution)/shard_map/cut_quarters/pallas_call | solution.py:252
  25.7 3.5 %collective-permute-start = (bf16[2,896,128]{2,1,0:T(8,128)(2,1)}, bf16[2,896,128]{2,1,0:T(8,128)(2,1)S(1)}, u32[]{:S(2)}, u32[]{:S(2)}) collective-permute-start(bf16[2,896,128]{2,1,0:T(8,128)(2,1)} %get-tuple-element.32), channel_id=1, source_target_pairs={{0,128},{128,256},{256,384},{384,0},{1,129},{129,257},{257,385},{3... | collective-permute-start | bytes 1376264 | tf_op jit(solution)/shard_map/ppermute | solution.py:229
  29.1 3.6 %collective-permute-start.1 = (bf16[2,896,128]{2,1,0:T(8,128)(2,1)}, bf16[2,896,128]{2,1,0:T(8,128)(2,1)S(1)}, u32[]{:S(2)}, u32[]{:S(2)}) collective-permute-start(bf16[2,896,128]{2,1,0:T(8,128)(2,1)} %get-tuple-element.33), channel_id=1, source_target_pairs={{0,384},{128,0},{256,128},{384,256},{1,385},{129,1},{257,129},{385... | collective-permute-start | bytes 1376264 | tf_op jit(solution)/shard_map/ppermute | solution.py:229
  32.7 3.9 %collective-permute-start.2 = (bf16[2,896,128]{2,1,0:T(8,128)(2,1)}, bf16[2,896,128]{2,1,0:T(8,128)(2,1)S(1)}, u32[]{:S(2)}, u32[]{:S(2)}) collective-permute-start(bf16[2,896,128]{2,1,0:T(8,128)(2,1)} %get-tuple-element.34), channel_id=1, source_target_pairs={{0,256},{128,384},{256,0},{384,128},{1,257},{129,385},{257,1},{385... | collective-permute-start | bytes 1376264 | tf_op jit(solution)/shard_map/ppermute | solution.py:229
  36.6 2.6 %collective-permute-start.4 = (bf16[128,3584]{1,0:T(8,128)(2,1)}, bf16[128,3584]{1,0:T(8,128)(2,1)S(1)}, u32[]{:S(2)}, u32[]{:S(2)}) collective-permute-start(bf16[128,3584]{1,0:T(8,128)(2,1)} %bitcast.13), channel_id=1, source_target_pairs={{0,128},{128,256},{256,384},{384,0},{1,129},{129,257},{257,385},{3... | collective-permute-start | bytes 2752520 | tf_op jit(solution)/shard_map/ppermute | solution.py:229
  39.2 4.5 %collective-permute-start.5 = (bf16[128,3584]{1,0:T(8,128)(2,1)}, bf16[128,3584]{1,0:T(8,128)(2,1)S(1)}, u32[]{:S(2)}, u32[]{:S(2)}) collective-permute-start(bf16[128,3584]{1,0:T(8,128)(2,1)} %bitcast.13), channel_id=1, source_target_pairs={{0,384},{128,0},{256,128},{384,256},{1,385},{129,1},{257,129},{385... | collective-permute-start | bytes 2752520 | tf_op jit(solution)/shard_map/ppermute | solution.py:229
  43.7 0.0 collective-permute-done
  43.7 7.8 %collective-permute-done.1 = bf16[2,896,128]{2,1,0:T(8,128)(2,1)S(1)} collective-permute-done((bf16[2,896,128]{2,1,0:T(8,128)(2,1)}, bf16[2,896,128]{2,1,0:T(8,128)(2,1)S(1)}, u32[]{:S(2)}, u32[]{:S(2)}) %collective-permute-start.1) | collective-permute-done | bytes 458784 | tf_op jit(solution)/shard_map/ppermute | solution.py:229
  51.5 2.1 %collective-permute-done.2 = bf16[2,896,128]{2,1,0:T(8,128)(2,1)S(1)} collective-permute-done((bf16[2,896,128]{2,1,0:T(8,128)(2,1)}, bf16[2,896,128]{2,1,0:T(8,128)(2,1)S(1)}, u32[]{:S(2)}, u32[]{:S(2)}) %collective-permute-start.2) | collective-permute-done | bytes 458784 | tf_op jit(solution)/shard_map/ppermute | solution.py:229
  53.5 1.2 pad_maximum_fusion.w0_ref
  54.8 1.9 collective-permute-start.3
  56.7 13.5 %collective-permute-done.4 = bf16[128,3584]{1,0:T(8,128)(2,1)S(1)} collective-permute-done((bf16[128,3584]{1,0:T(8,128)(2,1)}, bf16[128,3584]{1,0:T(8,128)(2,1)S(1)}, u32[]{:S(2)}, u32[]{:S(2)}) %collective-permute-start.4) | collective-permute-done | bytes 917536 | tf_op jit(solution)/shard_map/ppermute | solution.py:229
  70.2 0.9 slice.8
  71.1 2.2 %collective-permute-start.6 = (bf16[64,3584]{1,0:T(8,128)(2,1)}, bf16[64,3584]{1,0:T(8,128)(2,1)S(1)}, u32[]{:S(2)}, u32[]{:S(2)}) collective-permute-start(bf16[64,3584]{1,0:T(8,128)(2,1)} %slice.8), channel_id=1, source_target_pairs={{0,128},{128,256},{256,384},{384,0},{1,129},{129,257},{257,385},{3... | collective-permute-start | bytes 1376264 | tf_op jit(solution)/shard_map/ppermute | solution.py:229
  73.4 0.0 collective-permute-done.5
  73.4 0.0 copy-start.6
  73.4 0.8 slice.9
  74.3 4.8 %collective-permute-start.7 = (bf16[64,3584]{1,0:T(8,128)(2,1)}, bf16[64,3584]{1,0:T(8,128)(2,1)}, u32[]{:S(2)}, u32[]{:S(2)}) collective-permute-start(bf16[64,3584]{1,0:T(8,128)(2,1)} %slice.9), channel_id=1, source_target_pairs={{0,384},{128,0},{256,128},{384,256},{1,385},{129,1},{257,129},{385... | collective-permute-start | bytes 1376264 | tf_op jit(solution)/shard_map/ppermute | solution.py:229
  79.0 2.2 %constant_dynamic-update-slice_fusion.4 = bf16[512,3584]{1,0:T(8,128)(2,1)} fusion(bf16[1,128,3584]{2,1,0:T(8,128)(2,1)} %param.11), kind=kLoop, calls=%fused_computation.5 | loop fusion | bytes 1835008
  81.2 0.0 copy-done.4
  81.2 0.0 copy-done.6
  81.2 0.0 collective-permute-done.3.w1_ref
  81.3 1.2 copy-done.1
  82.5 0.0 all-to-all-done
  82.5 0.0 copy-done.3
  82.5 1.6 copy-done.2
  84.2 4.3 %gate_up.1 = bf16[512,2048]{1,0:T(8,128)(2,1)S(1)} custom-call(s32[4]{0:T(128)S(1)} %copy-done.3, bf16[512,896]{1,0:T(8,128)(2,1)S(1)} %bitcast.21, bf16[4,2,896,128]{3,2,1,0:T(8,128)(2,1)S(1)} %pad_maximum_fusion.w0_ref, bf16[4,2,896,128]{3,2,1,0:T(8,128)(2,1)S(1)} %copy-done.2), custom_call_target="tpu_custom_call" | custom-call | tf_op jit(solution)/shard_map/gate_up/pallas_call | solution.py:157
  88.4 0.0 collective-permute-done.6
  88.5 0.0 collective-permute-done.7
  88.5 0.1 constant_dynamic-update-slice_fusion.3
  88.6 0.1 constant_dynamic-update-slice_fusion.2
  88.7 1.1 constant_dynamic-update-slice_fusion.w0_ref
  89.7 1.9 collective-permute-start.8
  91.7 31.2 %all_to_all.32.x_ref = bf16[4,128,2048]{2,1,0:T(8,128)(2,1)S(1)} all-to-all(bf16[4,128,2048]{2,1,0:T(8,128)(2,1)S(1)} %bitcast.19), channel_id=1, replica_groups=mesh['y'=4,'x'=4,'z'=16,'c'=2] {'y'}, dimensions={0} | all-to-all | bytes 4194304 | tf_op jit(solution)/shard_map/all_to_all | solution.py:237
  122.9 0.0 collective-permute-done.8.w1_ref
  122.9 5.1 %down_rows.1 = bf16[512,896]{1,0:T(8,128)(2,1)} custom-call(s32[4]{0:T(128)S(1)} %copy-done.3, bf16[4,128,2048]{2,1,0:T(8,128)(2,1)S(1)} %all_to_all.32.x_ref, bf16[512,3584]{1,0:T(8,128)(2,1)S(1)} %constant_dynamic-update-slice_fusion.w0_ref, bf16[512,3584]{1,0:T(8,128)(2,1)S(1)} %collective-permute-done.8.w1_ref), custom_call_target="tpu_custom_call" | custom-call | tf_op jit(solution)/shard_map/down_rows/pallas_call | solution.py:208
  128.0 15.1 %all-to-all-start.2 = ((bf16[64,8,896]{2,1,0:T(8,128)(2,1)}), bf16[64,8,896]{2,1,0:T(8,128)(2,1)S(1)}, u32[]{:S(2)}, u32[]{:S(2)}) async-start(bf16[64,8,896]{2,1,0:T(8,128)(2,1)} %bitcast.15), calls=%async_computation.2 | async-start | bytes 1835008 | tf_op jit(solution)/shard_map/all_to_all | solution.py:237
  143.1 0.0 copy-done.8
  143.1 0.1 copy.7.ids_ref
  143.2 0.0 copy-done.9
  143.2 0.1 copy.8.weight_ref
  143.3 47.5 %all-to-all-done.2 = bf16[64,8,896]{2,1,0:T(8,128)(2,1)S(1)} async-done(((bf16[64,8,896]{2,1,0:T(8,128)(2,1)}), bf16[64,8,896]{2,1,0:T(8,128)(2,1)S(1)}, u32[]{:S(2)}, u32[]{:S(2)}) %all-to-all-start.2) | async-done | bytes 917536 | tf_op jit(solution)/shard_map/all_to_all | solution.py:237
  190.8 0.9 combine_rows.1
  191.7 8.9 %all_to_all.33 = bf16[4,8,3584]{2,1,0:T(8,128)(2,1)S(1)} all-to-all(bf16[4,8,3584]{2,1,0:T(8,128)(2,1)S(1)} %combine_rows.1), channel_id=1, replica_groups=mesh['y'=4,'x'=4,'z'=16,'c'=2] {'y'}, dimensions={0} | all-to-all | bytes 458752 | tf_op jit(solution)/shard_map/all_to_all | solution.py:237
  200.6 0.7 copy.14
  (13 shorter events, 0.1 us)
Async XLA Ops:
  2.7 79.8 %all-to-all-start = ((bf16[64,8,896]{2,1,0:T(8,128)(2,1)}), bf16[64,8,896]{2,1,0:T(8,128)(2,1)S(1)}, u32[]{:S(2)}, u32[]{:S(2)}) async-start(bf16[64,8,896]{2,1,0:T(8,128)(2,1)} %bitcast.30), calls=%async_computation | async-start | bytes 1835008 | tf_op jit(solution)/shard_map/all_to_all | solution.py:237
  25.7 18.0 %collective-permute-start = (bf16[2,896,128]{2,1,0:T(8,128)(2,1)}, bf16[2,896,128]{2,1,0:T(8,128)(2,1)S(1)}, u32[]{:S(2)}, u32[]{:S(2)}) collective-permute-start(bf16[2,896,128]{2,1,0:T(8,128)(2,1)} %get-tuple-element.32), channel_id=1, source_target_pairs={{0,128},{128,256},{256,384},{384,0},{1,129},{129,257},{257,385},{3... | collective-permute-start | bytes 1376264 | tf_op jit(solution)/shard_map/ppermute | solution.py:229
  29.1 22.3 %collective-permute-start.1 = (bf16[2,896,128]{2,1,0:T(8,128)(2,1)}, bf16[2,896,128]{2,1,0:T(8,128)(2,1)S(1)}, u32[]{:S(2)}, u32[]{:S(2)}) collective-permute-start(bf16[2,896,128]{2,1,0:T(8,128)(2,1)} %get-tuple-element.33), channel_id=1, source_target_pairs={{0,384},{128,0},{256,128},{384,256},{1,385},{129,1},{257,129},{385... | collective-permute-start | bytes 1376264 | tf_op jit(solution)/shard_map/ppermute | solution.py:229
  32.7 20.8 %collective-permute-start.2 = (bf16[2,896,128]{2,1,0:T(8,128)(2,1)}, bf16[2,896,128]{2,1,0:T(8,128)(2,1)S(1)}, u32[]{:S(2)}, u32[]{:S(2)}) collective-permute-start(bf16[2,896,128]{2,1,0:T(8,128)(2,1)} %get-tuple-element.34), channel_id=1, source_target_pairs={{0,256},{128,384},{256,0},{384,128},{1,257},{129,385},{257,1},{385... | collective-permute-start | bytes 1376264 | tf_op jit(solution)/shard_map/ppermute | solution.py:229
  36.6 33.6 %collective-permute-start.4 = (bf16[128,3584]{1,0:T(8,128)(2,1)}, bf16[128,3584]{1,0:T(8,128)(2,1)S(1)}, u32[]{:S(2)}, u32[]{:S(2)}) collective-permute-start(bf16[128,3584]{1,0:T(8,128)(2,1)} %bitcast.13), channel_id=1, source_target_pairs={{0,128},{128,256},{256,384},{384,0},{1,129},{129,257},{257,385},{3... | collective-permute-start | bytes 2752520 | tf_op jit(solution)/shard_map/ppermute | solution.py:229
  39.2 34.2 %collective-permute-start.5 = (bf16[128,3584]{1,0:T(8,128)(2,1)}, bf16[128,3584]{1,0:T(8,128)(2,1)S(1)}, u32[]{:S(2)}, u32[]{:S(2)}) collective-permute-start(bf16[128,3584]{1,0:T(8,128)(2,1)} %bitcast.13), channel_id=1, source_target_pairs={{0,384},{128,0},{256,128},{384,256},{1,385},{129,1},{257,129},{385... | collective-permute-start | bytes 2752520 | tf_op jit(solution)/shard_map/ppermute | solution.py:229
  53.5 29.0 %copy-start.3 = (s32[4]{0:T(128)S(1)}, s32[4]{0:T(128)}, u32[]{:S(2)}) copy-start(s32[4]{0:T(128)} %pad_add_fusion.q_ref) | copy-start | bytes 52
  54.8 26.5 %collective-permute-start.3 = (bf16[4,2,896,128]{3,2,1,0:T(8,128)(2,1)S(1)}, bf16[4,2,896,128]{3,2,1,0:T(8,128)(2,1)S(1)}, u32[]{:S(2)}, u32[]{:S(2)}) collective-permute-start(bf16[4,2,896,128]{3,2,1,0:T(8,128)(2,1)S(1)} %pad_maximum_fusion.w0_ref), channel_id=1, source_target_pairs={{0,1},{1,0},{2,3},{3,2},{4,5},{5,4},{6,7},{7,6},{8,9},{9,8},{10,11... | collective-permute-start | bytes 5505032 | tf_op jit(solution)/shard_map/ppermute | solution.py:233
  70.2 11.0 %copy-start.4 = (bf16[128,3584]{1,0:T(8,128)(2,1)}, bf16[128,3584]{1,0:T(8,128)(2,1)S(1)}, u32[]{:S(2)}) copy-start(bf16[128,3584]{1,0:T(8,128)(2,1)S(1)} %collective-permute-done.4) | copy-start | bytes 2752516
  71.1 17.3 %collective-permute-start.6 = (bf16[64,3584]{1,0:T(8,128)(2,1)}, bf16[64,3584]{1,0:T(8,128)(2,1)S(1)}, u32[]{:S(2)}, u32[]{:S(2)}) collective-permute-start(bf16[64,3584]{1,0:T(8,128)(2,1)} %slice.8), channel_id=1, source_target_pairs={{0,128},{128,256},{256,384},{384,0},{1,129},{129,257},{257,385},{3... | collective-permute-start | bytes 1376264 | tf_op jit(solution)/shard_map/ppermute | solution.py:229
  73.4 7.8 %copy-start.6 = (bf16[128,3584]{1,0:T(8,128)(2,1)}, bf16[128,3584]{1,0:T(8,128)(2,1)S(1)}, u32[]{:S(2)}) copy-start(bf16[128,3584]{1,0:T(8,128)(2,1)S(1)} %collective-permute-done.5) | copy-start | bytes 2752516
  74.3 14.2 %collective-permute-start.7 = (bf16[64,3584]{1,0:T(8,128)(2,1)}, bf16[64,3584]{1,0:T(8,128)(2,1)}, u32[]{:S(2)}, u32[]{:S(2)}) collective-permute-start(bf16[64,3584]{1,0:T(8,128)(2,1)} %slice.9), channel_id=1, source_target_pairs={{0,384},{128,0},{256,128},{384,256},{1,385},{129,1},{257,129},{385... | collective-permute-start | bytes 1376264 | tf_op jit(solution)/shard_map/ppermute | solution.py:229
  81.2 1.3 copy-start.1
  82.5 6.0 %copy-start = (bf16[512,3584]{1,0:T(8,128)(2,1)S(1)}, bf16[512,3584]{1,0:T(8,128)(2,1)}, u32[]{:S(2)}) copy-start(bf16[512,3584]{1,0:T(8,128)(2,1)} %constant_dynamic-update-slice_fusion.4) | copy-start | bytes 11010052
  82.5 1.7 copy-start.2
  84.2 4.3 %copy-start.5 = (bf16[128,3584]{1,0:T(8,128)(2,1)S(1)}, bf16[128,3584]{1,0:T(8,128)(2,1)}, u32[]{:S(2)}) copy-start(bf16[128,3584]{1,0:T(8,128)(2,1)} %copy-done.4) | copy-start | bytes 2752516
  84.2 4.4 %copy-start.7 = (bf16[128,3584]{1,0:T(8,128)(2,1)S(1)}, bf16[128,3584]{1,0:T(8,128)(2,1)}, u32[]{:S(2)}) copy-start(bf16[128,3584]{1,0:T(8,128)(2,1)} %copy-done.6) | copy-start | bytes 2752516
  89.7 33.2 %collective-permute-start.8 = (bf16[512,3584]{1,0:T(8,128)(2,1)S(1)}, bf16[512,3584]{1,0:T(8,128)(2,1)S(1)}, u32[]{:S(2)}, u32[]{:S(2)}) collective-permute-start(bf16[512,3584]{1,0:T(8,128)(2,1)S(1)} %constant_dynamic-update-slice_fusion.w0_ref), channel_id=1, source_target_pairs={{0,1},{1,0},{2,3},{3,2},{4,5},{5,4},{6,7},{7,6},{8,9},{9,8},{10,11... | collective-permute-start | bytes 11010056 | tf_op jit(solution)/shard_map/ppermute | solution.py:233
  122.9 20.2 %copy-start.8 = (s32[32,8]{0,1:T(8,128)S(1)}, s32[32,8]{0,1:T(8,128)}, u32[]{:S(2)}) copy-start(s32[32,8]{0,1:T(8,128)} %param.7) | copy-start | bytes 3076
  122.9 20.3 %copy-start.9 = (f32[32,8]{0,1:T(8,128)S(1)}, f32[32,8]{0,1:T(8,128)}, u32[]{:S(2)}) copy-start(f32[32,8]{0,1:T(8,128)} %param.8) | copy-start | bytes 3076
  128.0 62.8 %all-to-all-start.2 = ((bf16[64,8,896]{2,1,0:T(8,128)(2,1)}), bf16[64,8,896]{2,1,0:T(8,128)(2,1)S(1)}, u32[]{:S(2)}, u32[]{:S(2)}) async-start(bf16[64,8,896]{2,1,0:T(8,128)(2,1)} %bitcast.15), calls=%async_computation.2 | async-start | bytes 1835008 | tf_op jit(solution)/shard_map/all_to_all | solution.py:237
